TPU v7x, 256 devices: a whole 4x4x8 slice. The times are simulated.
256 devices in a mesh: ctx: 64 (over y, z, x_lo), head: 4 (over x_hi, core).
Axes of the slice: x: 4 (x_hi: 2, x_lo: 2; x = x_hi * 2 + x_lo), y: 4, z: 8, core: 2. Of those that a mesh axis runs over, the one named last changes fastest.
Arguments:
- queries: bfloat16 [128, 8192], P('ctx', 'head'), may hold values from -32 to 32
- keys: bfloat16 [131072, 1024], P('ctx', 'head'), may hold values from -16 to 16
- values: bfloat16 [131072, 1024], P('ctx', 'head'), may hold values from -20 to 20
- norm_gain: bfloat16 [8192], P('head'), may hold values from 0.099609375 to 1.8984375
- adapter: bfloat16 [1024, 8192], P('ctx', 'head'), may hold values from -0.0625 to 0.0625
- source_row: int32 [128], replicated, may hold values from 0 to 127, each once
- cotangent: bfloat16 [128, 1024], P('ctx'), may hold values from -16 to 16
Outputs:
- student_out: float32 [128, 1024], P('ctx')
- adapter_grad: float32 [1024, 8192], P('ctx', 'head')
Inputs may be any that keep to these rules, and one draw needn't show every extreme that they name: `source_row`: each response row is read by exactly one student token.
All inputs are finite; a program needn't handle non-finite values.
Results may differ from a plain program's by a relative error of at most 0.015.
Values may be sent and summed in bfloat16 or wider, within the bound.
A program may use at most 192 MiB of HBM per device.

v0:
```python
import jax
import jax.numpy as jnp
from jax import lax
from jax.sharding import PartitionSpec as P

H = 64
HD = 128


def combined_all(part, axis, combine):
    gathered = jax.tree.map(lambda a: lax.all_gather(a, axis), part)

    def take(source):
        return jax.tree.map(lambda a: lax.dynamic_index_in_dim(a, source, 0, False), gathered)

    return lax.fori_loop(
        1, lax.axis_size(axis), lambda source, state: combine(state, take(source)), take(0)
    )


def contract_last(left, right):
    return lax.dot_general(
        left, right, (((1,), (1,)), ((), ())), preferred_element_type=jnp.float32
    )


def head_attention(query_rows, key_rows, value_rows):
    row_count = query_rows.shape[0]
    block_rows = min(512, row_count)
    grouped = query_rows.reshape(row_count // block_rows, block_rows, query_rows.shape[1])

    def one_block(segment):
        scores = contract_last(segment, key_rows) * HD ** (-0.5)
        maxima = jnp.max(scores, axis=1)
        weights = jnp.exp(scores - maxima[:, None])
        totals = jnp.sum(weights, axis=1)
        partial_value = jnp.dot(
            weights.astype(jnp.bfloat16), value_rows, preferred_element_type=jnp.float32
        )
        return (partial_value, maxima, totals)

    partial_value, maxima, totals = lax.map(one_block, grouped)
    return (
        partial_value.reshape(row_count, HD),
        maxima.reshape(row_count),
        totals.reshape(row_count),
    )


def local_attention(every_query, keys, values):
    row_count = every_query.shape[0]
    kv_local = keys.shape[1] // HD
    group = every_query.shape[1] // HD // kv_local
    head_view = every_query.reshape(row_count, kv_local, group * HD)
    partials, maxima_list, totals_list = ([], [], [])
    for head_slot in range(kv_local):
        query_rows = head_view[:, head_slot].reshape(row_count * group, HD)
        key_rows = keys[:, head_slot * HD : (head_slot + 1) * HD]
        value_rows = values[:, head_slot * HD : (head_slot + 1) * HD]
        partial_value, maxima, totals = head_attention(query_rows, key_rows, value_rows)
        partials.append(partial_value.reshape(row_count, group * HD))
        maxima_list.append(maxima.reshape(row_count, group))
        totals_list.append(totals.reshape(row_count, group))
    return (
        jnp.concatenate(partials, axis=1),
        jnp.concatenate(maxima_list, axis=1),
        jnp.concatenate(totals_list, axis=1),
    )


def join_carries(first, second):
    first_out, first_max, first_sum = first
    second_out, second_max, second_sum = second
    top_max = jnp.maximum(first_max, second_max)
    first_weight = jnp.exp(first_max - top_max)
    second_weight = jnp.exp(second_max - top_max)
    row_count, head_count = top_max.shape
    merged = (
        first_out.reshape(row_count, head_count, HD) * first_weight[:, :, None]
        + second_out.reshape(row_count, head_count, HD) * second_weight[:, :, None]
    )
    return (
        merged.reshape(row_count, head_count * HD),
        top_max,
        first_sum * first_weight + second_sum * second_weight,
    )


def finish_rows(summed, totals):
    row_count, head_count = totals.shape
    return (
        (summed.reshape(row_count, head_count, HD) / totals[:, :, None])
        .reshape(row_count, head_count * HD)
        .astype(jnp.bfloat16)
    )


def prepare_rows(rows, norm_gain):
    widened = rows.astype(jnp.float32)
    power = jnp.sum(widened * widened, axis=1)
    gained = (widened * norm_gain.astype(jnp.float32)[None, :]).astype(jnp.bfloat16)
    return (gained, power)


def slope_of(pre_acts):
    sigmoid_val = jax.nn.sigmoid(pre_acts)
    return sigmoid_val * (1.0 + pre_acts * (1.0 - sigmoid_val))


def local(queries, keys, values, norm_gain, adapter, source_row, cotangent):
    rows_local = queries.shape[0]
    every_query = lax.all_gather(queries, "ctx", axis=0, tiled=True)
    row_total = every_query.shape[0]
    partials, maxima, totals = local_attention(every_query, keys, values)
    summed, top_max, weight_sum = combined_all((partials, maxima, totals), "ctx", join_carries)
    hidden_all = finish_rows(summed, weight_sum)
    own_index = lax.axis_index("ctx")
    own_rows = lax.dynamic_slice_in_dim(source_row, own_index * rows_local, rows_local)
    gained, power = prepare_rows(jnp.take(hidden_all, own_rows, axis=0), norm_gain)
    pre_part = contract_last(gained, lax.all_gather(adapter, "ctx", axis=0, tiled=True))
    pre_sum, power_sum = lax.psum((pre_part, power), "head")
    scale = lax.rsqrt(power_sum / (H * HD) + 1e-05)
    pre_acts = scale[:, None] * pre_sum
    student_out = jax.nn.silu(pre_acts)
    slope = (cotangent.astype(jnp.float32) * slope_of(pre_acts) * scale[:, None]).astype(
        jnp.bfloat16
    )
    adapter_grad = lax.psum_scatter(
        lax.dot_general(
            slope, gained, (((0,), (0,)), ((), ())), preferred_element_type=jnp.float32
        ),
        "ctx",
        scatter_dimension=0,
        tiled=True,
    ) * row_total ** (-0.5)
    return (student_out, adapter_grad)


def solution(mesh):
    return jax.shard_map(
        local,
        mesh=mesh,
        in_specs=(
            P("ctx", "head"),
            P("ctx", "head"),
            P("ctx", "head"),
            P("head"),
            P("ctx", "head"),
            P(),
            P("ctx", None),
        ),
        out_specs=(P("ctx", None), P("ctx", "head")),
        check_vma=False,
    )
```

profile of v0, /device:TPU:0, one launch (start us, length us, event | category | flops | bytes accessed | tf_op | source)
XLA Modules:
  0.0 2296.4 jit_solution(10967840714998780104)
XLA Ops:
  7.2 160.4 %all-gather.3 = bf16[64,2,2048]{2,1,0:T(2,128)(2,1)S(1)} all-gather(bf16[1,2,2048]{2,1,0:T(2,128)(2,1)} %bitcast.104), channel_id=1, replica_groups=mesh['ctx'=64,'head'=4] {'ctx'}, dimensions={0}, use_global_device_ids=true | all-gather | bytes 532480 | tf_op jit(solution)/shard_map/all_gather | solution.py:112
  172.1 5.1 while.47
  177.4 5.1 while.48
  184.9 169.3 %all-gather.2 = f32[8192,16]{0,1:T(8,128)S(1)} all-gather(f32[128,16]{0,1:T(8,128)S(1)} %pad_maximum_fusion.2), channel_id=4, replica_groups=mesh['ctx'=64,'head'=4] {'ctx'}, dimensions={0}, use_global_device_ids=true | all-gather | bytes 532480 | tf_op jit(solution)/shard_map/all_gather | solution.py:11
  354.3 2.6 copy.32
  357.2 168.6 %all-gather.1 = f32[8192,16]{0,1:T(8,128)S(1)} all-gather(f32[128,16]{0,1:T(8,128)S(1)} %pad_maximum_fusion.1), channel_id=3, replica_groups=mesh['ctx'=64,'head'=4] {'ctx'}, dimensions={0}, use_global_device_ids=true | all-gather | bytes 532480 | tf_op jit(solution)/shard_map/all_gather | solution.py:11
  525.8 2.6 copy.31
  528.8 1100.0 %all-gather.9.cloned.1.call-done = f32[8192,2048]{1,0:T(8,128)} async-done(((f32[128,2048]{1,0:T(8,128)}), f32[8192,2048]{1,0:T(8,128)}) %all-gather.9.cloned.1.call-update) | async-done | bytes 67108880 | tf_op jit(solution)/shard_map/all_gather | solution.py:11
  1630.0 249.3 %while.49 = (s32[]{:T(128)}, f32[128,2048]{1,0:T(8,128)S(1)}, f32[128,16]{1,0:T(8,128)S(1)}, f32[128,16]{1,0:T(8,128)S(1)}, f32[64,128,16]{2,1,0:T(8,128)}, /*in...) while((s32[]{:T(128)}, f32[128,2048]{1,0:T(8,128)S(1)}, ...), condition=%wide.region_9.10_spmd, body=%wide.region_8.9_spmd.sunk | while | flops 798725 | bytes 7422103 | solution.py:16
  1655.4 2.3 fusion.77
  1698.9 2.3 fusion.77
  1706.8 2.3 fusion.77
  1750.4 2.3 fusion.77
  1758.3 2.3 fusion.77
  1801.8 2.3 fusion.77
  1809.7 2.3 fusion.77
  1829.5 2.3 fusion.77
  1853.3 2.3 fusion.77
  1873.0 2.3 fusion.77
  1880.9 60.1 %all-gather.7.cloned.1.call-done = bf16[1024,2048]{1,0:T(8,128)(2,1)} async-done(((bf16[16,2048]{1,0:T(8,128)(2,1)}), bf16[1024,2048]{1,0:T(8,128)(2,1)}) %all-gather.7.cloned.1.call-update) | async-done | bytes 4194320 | tf_op jit(solution)/shard_map/all_gather | solution.py:120
  1941.0 3.4 fusion.43
  1944.4 7.4 all-reduce
  1951.8 4.6 fusion.40
  1957.1 331.2 %reduce-scatter.2.cloned.1.call-done = f32[16,2048]{1,0:T(8,128)} async-done(((f32[1024,2048]{1,0:T(8,128)}), f32[16,2048]{1,0:T(8,128)}) %reduce-scatter.2.cloned.1.call-update) | async-done | bytes 131088 | tf_op jit(solution)/shard_map/reduce_scatter | solution.py:128
  (313 shorter events, 247.5 us)
Async XLA Ops:
  7.2 1621.5 %all-gather.9.cloned.1.call-start = ((), (), s32[]{:S(2)}) async-start(), calls=%async_computation.3 | async-start | bytes 68157440 | tf_op jit(solution)/shard_map/all_gather | solution.py:11
  183.8 1757.2 %all-gather.7.cloned.1.call-start = ((), (), s32[]{:S(2)}) async-start(), calls=%async_computation.1 | async-start | bytes 4259840 | tf_op jit(solution)/shard_map/all_gather | solution.py:120
  184.6 2103.8 %reduce-scatter.2.cloned.1.call-start = ((), (), s32[]{:S(2)}) async-start(), calls=%async_computation.2 | async-start | bytes 8519680 | tf_op jit(solution)/shard_map/reduce_scatter | solution.py:128
  354.3 174.4 %copy-start.2 = (s32[128]{0:T(128)S(1)}, s32[128]{0:T(128)}, u32[]{:S(2)}) copy-start(s32[128]{0:T(128)} %param.18) | copy-start | bytes 1540
  354.3 174.5 %copy-start.1 = (bf16[2048]{0:T(1024)(128)(2,1)S(1)}, bf16[2048]{0:T(1024)(128)(2,1)}, u32[]{:S(2)}) copy-start(bf16[2048]{0:T(1024)(128)(2,1)} %param.16) | copy-start | bytes 12292
  1879.3 72.5 %copy-start = (bf16[2,1024]{1,0:T(2,128)(2,1)S(1)}, bf16[2,1024]{1,0:T(2,128)(2,1)}, u32[]{:S(2)}) copy-start(bf16[2,1024]{1,0:T(2,128)(2,1)} %param.19) | copy-start | bytes 12292
Sparse Core Ops, SparseCore 0:
  183.9 1444.7 all-gather.8
  1630.5 310.4 all-gather.6
  1956.6 331.7 reduce-scatter.1
where the time goes:
time: 2300 us
  waiting for transfers between devices  1490 us (65%)
  blocking collectives  506 us (22%)
  other arithmetic  213 us (9%)
  local copies, waits for them, and re-layouts  55.5 us (2%)
    all_gather x1, waiting for transfers between devices, combined_all(): gathered = jax.tree.map(lambda a: lax.all_gather(a, axis), part)  1100 us
    all_gather x2, blocking collectives, combined_all(): gathered = jax.tree.map(lambda a: lax.all_gather(a, axis), part)  338 us
    reduce_scatter x1, waiting for transfers between devices, local(): lax.psum_scatter(lax.dot_general(slope, gained, (((0,), (0,)), ((), ())),...  331 us
    all_gather x1, blocking collectives, local(): every_query = lax.all_gather(queries, 'ctx', axis=0, tiled=True)  160 us
    add x63, other arithmetic, join_carries(): first_out.reshape(row_count, head_count, HD) * first_weight[:, :, None]  146 us
    all_gather x1, waiting for transfers between devices, local(): lax.all_gather(adapter, 'ctx', axis=0, tiled=True)  60.1 us
    add x63, other arithmetic, join_carries(): first_sum * first_weight + second_sum * second_weight  59.4 us
  transfers between devices with their start and end apart: 3, of which 3 were waited for; matrix products, arithmetic and copies ran while one was open for 11% of the time, Pallas kernels for 0%

commit v1 on v0

v1 whole, which is shorter than its diff:
```python
import functools

import jax
import jax.numpy as jnp
from jax import lax
from jax.experimental import pallas as pl
from jax.experimental.pallas import tpu as pltpu
from jax.sharding import PartitionSpec as P

H = 64
HD = 128
GROUP = 8
LANES = 128
LOG2E = 1.4426950408889634
YN, ZN, XN = 4, 8, 2

F32 = jnp.float32
BF16 = jnp.bfloat16
MESH = pl.DeviceIdType.MESH


def iota(shape, axis):
    return lax.broadcasted_iota(jnp.int32, shape, axis)


def nn(left, right):
    return lax.dot_general(left, right, (((1,), (0,)), ((), ())), preferred_element_type=F32)


def div(a, n):
    return a // n if isinstance(a, int) else a >> (n.bit_length() - 1)


def mod(a, n):
    return a % n if isinstance(a, int) else a & (n - 1)


def regroup(outer, zn):
    size = outer * zn * 2
    row, col = iota((size, 1), 0), iota((size, size), 1)
    head, rest = div(row, 2 * zn), mod(row, 2 * zn)
    return (col == div(rest, 2) * (2 * outer) + head * 2 + mod(rest, 2)).astype(F32).astype(BF16)


def row_of(position, sizes):
    yn, zn, xn = sizes
    pair, block = div(position, 2), div(position, 2 * zn)
    ctx = (div(block, xn) * zn + mod(pair, zn)) * xn + mod(block, xn)
    return 2 * ctx + mod(position, 2)


def split3(value):
    high = value.astype(BF16)
    rest = value - high.astype(F32)
    middle = rest.astype(BF16)
    return high, middle, (rest - middle.astype(F32)).astype(BF16)


def kernel(sizes, heads, eps_div, q_hbm, k_hbm, v_hbm, gain_hbm, ad_hbm, src_hbm, cot_hbm,
           stu_ref, grad_ref,
           q_ref, gain_ref, src_ref, cot_ref, kbuf, k_t, vaug, qall, osend, orecv, zsend, zrecv,
           hz, hall, gall, mpre, squares, hx, s_even, s_odd, regroup_h, cz, cg, call, cot_t, mpre_t, st1s, st1r,
           adp, ad_t,
           loc_sem, zq_s, zq_r, q2_s, q2_r, zc_s, zc_r, c2_s, c2_r, o_s, o_r,
           zr_s, zr_r, hz_s, hz_r, h2_s, h2_r, hx_s, hx_r, s1_s, s1_r, za_s, za_r):
    sbuf = (s_even, s_odd)
    yn, zn, xn = sizes
    nb = yn * xn
    tb = 2 * zn
    rows = nb * tb
    kvl = k_hbm.shape[1] // HD
    nh = kvl * GROUP
    kr = GROUP * 2
    cpd = ad_hbm.shape[0]
    per_group = LANES // cpd
    aw = zn * xn * cpd
    groups = cot_hbm.shape[1] // LANES

    ctx = lax.axis_index("ctx")
    hd = lax.axis_index("head")
    y = div(ctx, zn * xn)
    z = mod(div(ctx, xn), zn)
    x = mod(ctx, xn)
    b = y * xn + x

    def at(y_, z_, x_):
        return ((y_ * zn + z_) * xn + x_, hd)

    def z_plus(d):
        return mod(z + d, zn)

    ring = sorted(range(1, zn), key=lambda d: -min(d, zn - d))

    def z_dev(d):
        return at(y, z_plus(d), x)

    def steps(i):
        far, turn = div(i, yn), mod(i, yn)
        if isinstance(i, int):
            near = (0, 1, 3, 2)[turn] if yn == 4 else turn
            return (near if far == 0 else (2, 1, 3, 0)[turn] if yn == 4 else yn - 1 - turn), far
        if yn == 4:
            first = jnp.where(turn == 2, 3, jnp.where(turn == 3, 2, turn))
            second = jnp.where(turn == 0, 2, jnp.where(turn == 1, 1, jnp.where(turn == 2, 3, 0)))
        else:
            first, second = turn, yn - 1 - turn
        return jnp.where(far == 0, first, second), far

    def plus(i):
        dy, dx = steps(i)
        return mod(y + dy, yn), mod(x + dx, xn)

    def minus(i):
        dy, dx = steps(i)
        return mod(y + yn - dy, yn), mod(x + xn - dx, xn)

    def plus_dev(i):
        py, px = plus(i)
        return at(py, z, px)

    def minus_dev(i):
        py, px = minus(i)
        return at(py, z, px)

    def rcopy(src, dst, ssem, rsem, dev):
        return pltpu.make_async_remote_copy(
            src_ref=src, dst_ref=dst, send_sem=ssem, recv_sem=rsem, device_id=dev, device_id_type=MESH
        )

    q_load = pltpu.make_async_copy(q_hbm, q_ref, loc_sem.at[0])
    cot_load = pltpu.make_async_copy(cot_hbm, cot_ref, loc_sem.at[1])
    k_load = pltpu.make_async_copy(k_hbm, kbuf, loc_sem.at[2])
    own_ad = pl.ds(pl.multiple_of((z * xn + x) * cpd, cpd), cpd)
    ad_load = pltpu.make_async_copy(ad_hbm, adp.at[own_ad], loc_sem.at[3])
    late_loads = [
        pltpu.make_async_copy(gain_hbm, gain_ref, loc_sem.at[4]),
        pltpu.make_async_copy(src_hbm, src_ref, loc_sem.at[5]),
    ]
    for k in range(kvl):
        late_loads.append(
            pltpu.make_async_copy(
                v_hbm.at[:, k * HD : (k + 1) * HD], vaug.at[k, :, 0:HD], loc_sem.at[6 + k]
            )
        )
    for load in [q_load, cot_load, k_load, ad_load] + late_loads:
        load.start()

    barrier = pltpu.get_barrier_semaphore()
    partners = (
        [z_dev(d) for d in range(1, zn)]
        + [plus_dev(i) for i in range(1, nb)]
        + [(ctx, mod(hd + e, heads)) for e in range(1, heads)]
    )
    for dev in partners:
        pl.semaphore_signal(barrier, inc=1, device_id=dev, device_id_type=MESH)

    q_load.wait()
    qf = q_ref[...].astype(F32)
    for k in range(kvl):
        qall[k * nb, pl.ds(z, 1)] = jnp.concatenate(
            [qf[:, (k * GROUP + h) * HD : (k * GROUP + h + 1) * HD] for h in range(GROUP)], axis=0
        ).astype(BF16)[None]
    cot_load.wait()
    cf = cot_ref[...].astype(F32)
    cz[pl.ds(z, 1)] = jnp.concatenate(
        [cf[:, g * LANES : (g + 1) * LANES] for g in range(groups)], axis=0
    ).astype(BF16)[None]
    pl.semaphore_wait(barrier, len(partners))

    def z_group(make):
        copies = {d: make(d) for d in ring}
        for copy in copies.values():
            copy.start()
        return copies

    def received(copies):
        for copy in copies.values():
            copy.wait_recv()

    def sent(*groups_of_copies):
        for copies in groups_of_copies:
            for copy in copies.values():
                copy.wait_send()

    zq = [
        z_group(
            lambda d, k=k: rcopy(
                qall.at[k * nb, z], qall.at[k * nb, z], zq_s.at[k * zn + d], zq_r.at[k * zn + d], z_dev(d)
            )
        )
        for k in range(kvl)
    ]
    zc = z_group(lambda d: rcopy(cz.at[z], cz.at[z], zc_s.at[d], zc_r.at[d], z_dev(d)))

    k_load.wait()
    for k in range(kvl):
        k_t[k] = kbuf[:, k * HD : (k + 1) * HD].astype(F32).T.astype(BF16)
    for k in range(kvl):
        vaug[k, :, HD : 2 * HD] = jnp.ones((vaug.shape[1], HD), BF16)

    def q_copy(j, i):
        return rcopy(qall.at[j - i], qall.at[j], q2_s.at[j], q2_r.at[j], plus_dev(i))

    for k in range(kvl):
        received(zq[k])
        for i in range(1, nb):
            q_copy(k * nb + i, i).start()

    for d in range(zn):
        for e in range(1, xn):
            other = pl.multiple_of((d * xn + mod(x + e, xn)) * cpd, cpd)
            adp[pl.ds(other, cpd), :] = jnp.zeros((cpd, nh * HD), BF16)
    st1s[...] = jnp.zeros_like(st1s)
    ad_load.wait()
    za = z_group(lambda d: rcopy(adp.at[own_ad], adp.at[own_ad], za_s.at[d], za_r.at[d], z_dev(d)))
    for load in late_loads:
        load.wait()

    factor = (HD ** -0.5) * LOG2E
    qrows = zn * kr
    eye = iota((qrows, LANES), 0) == iota((qrows, LANES), 1)

    def stat_tile(row):
        high, middle, low = split3(row)
        line = iota((kr, LANES), 0)
        tile = jnp.where(line == 0, high.astype(F32), jnp.where(line == 1, middle.astype(F32), low.astype(F32)))
        return jnp.where(line < 3, tile, 0.0).astype(BF16)

    def stat_row(tile):
        wide = tile.astype(F32)
        return wide[0:1, :] + wide[1:2, :] + wide[2:3, :]

    def score(j, buf):
        buf[...] = nn(qall[j].reshape(qrows, HD), k_t[div(j, nb)])

    def weigh(j, k, buf):
        m = jnp.max(buf[...], axis=1, keepdims=True)
        p = jnp.exp2((buf[...] - m) * factor).astype(BF16)
        oa = nn(p, vaug[k])
        total = oa[:, HD : 2 * HD]
        o = oa[:, 0:HD] / total
        osend[j, 0:zn] = o.astype(BF16).reshape(zn, kr, HD)
        lse = m * factor + jnp.log2(total)
        osend[j, zn] = stat_tile(jnp.sum(jnp.where(eye, lse, 0.0), axis=0, keepdims=True))

    def o_copy(j, i):
        return rcopy(osend.at[j], orecv.at[j], o_s.at[j], o_r.at[j], minus_dev(i))

    def attend(k):
        def body(t, carry):
            first, second, third = 2 * t, 2 * t + 1, jnp.minimum(2 * t + 2, kvl * nb - 1)
            q_copy(second, mod(second, nb)).wait_recv()
            score(second, sbuf[1])
            weigh(first, k, sbuf[0])

            @pl.when(mod(first, nb) > 0)
            def _():
                o_copy(first, mod(first, nb)).start()

            @pl.when(mod(2 * t + 2, nb) > 0)
            def _():
                q_copy(third, mod(third, nb)).wait_recv()

            score(third, sbuf[0])
            weigh(second, k, sbuf[1])
            o_copy(second, mod(second, nb)).start()
            return carry

        return body

    def combine(k):
        for i in range(1, nb):
            o_copy(k * nb + i, i).wait_recv()
        parts = [(osend if i == 0 else orecv).at[k * nb + i] for i in range(nb)]
        stats = [stat_row(part[zn]) for part in parts]
        top = functools.reduce(jnp.maximum, stats)
        weights = [jnp.exp2(st - top) for st in stats]
        weight_sum = functools.reduce(jnp.add, weights)
        inverse = 1.0 / weight_sum
        acc = jnp.zeros((qrows, HD), F32)
        for i in range(nb):
            share = jnp.where(eye, weights[i] * inverse, 0.0)[:, 0:qrows].astype(BF16)
            acc = acc + nn(share, parts[i][0:zn].reshape(qrows, HD))
        zsend[k, :, 0:kr, :] = acc.astype(BF16).reshape(zn, kr, HD)
        tile = stat_tile(top + jnp.log2(weight_sum))
        for d in range(zn):
            zsend[k, d, kr : 2 * kr, :] = tile
        return z_group(
            lambda d: rcopy(
                zsend.at[k, z_plus(d)], zrecv.at[k, d], zr_s.at[k * zn + d], zr_r.at[k * zn + d], z_dev(d)
            )
        )

    mine = iota((kr, LANES), 1) == iota((kr, LANES), 0) + z * kr

    def settle(k, copies):
        received(copies)
        parts = [zsend[k, z]] + [zrecv[k, d] for d in range(1, zn)]
        stats = [stat_row(part[kr : 2 * kr, :]) for part in parts]
        top = functools.reduce(jnp.maximum, stats)
        weights = [jnp.exp2(st - top) for st in stats]
        inverse = 1.0 / functools.reduce(jnp.add, weights)
        acc = jnp.zeros((kr, HD), F32)
        for d in range(zn):
            column = jnp.sum(jnp.where(mine, weights[d] * inverse, 0.0), axis=1, keepdims=True)
            acc = acc + column * parts[d][0:kr, :].astype(F32)
        hz[k, pl.ds(z, 1)] = acc.astype(BF16)[None]
        return z_group(
            lambda d: rcopy(hz.at[k, z], hz.at[k, z], hz_s.at[k * zn + d], hz_r.at[k * zn + d], z_dev(d))
        )

    def spread(k, copies):
        received(copies)
        pieces = nn(regroup_h[...], hz[k].reshape(zn * kr, HD)).astype(BF16)
        for h in range(GROUP):
            hall[k, pl.ds(b, 1), :, h * HD : (h + 1) * HD] = pieces[h * tb : (h + 1) * tb, :][None]
        copies = {
            i: rcopy(hall.at[k, b], hall.at[k, b], h2_s.at[k * nb + i], h2_r.at[k * nb + i], plus_dev(i))
            for i in range(1, nb)
        }
        for copy in copies.values():
            copy.start()
        return copies

    def project(k, copies):
        gain = gain_ref[...].astype(F32)
        for i in range(nb):
            if i > 0:
                copies[i].wait_recv()
            my, mx = minus(i)
            there = my * xn + mx
            hidden = hall[k, there].astype(F32)
            lines = pl.ds(pl.multiple_of(there * tb, tb), tb)
            partial = jnp.zeros((tb, HD), F32)
            for h in range(GROUP):
                piece = hidden[:, h * HD : (h + 1) * HD]
                partial = partial + piece * piece
                head = k * GROUP + h
                gall[lines, head * HD : (head + 1) * HD] = (piece * gain[head : head + 1, :]).astype(BF16)
            squares[lines, :] = partial if k == 0 else squares[lines, :] + partial
        width = GROUP * HD
        part = nn(gall[:, k * width : (k + 1) * width], ad_t[k * width : (k + 1) * width, :])
        mpre[...] = part if k == 0 else mpre[...] + part

    def turn_adapter(k):
        for h in range(k * GROUP, (k + 1) * GROUP):
            for first in range(0, aw, LANES):
                ad_t[h * HD : (h + 1) * HD, first : first + LANES] = (
                    adp[first : first + LANES, h * HD : (h + 1) * HD].astype(F32).T.astype(BF16)
                )

    score(0, sbuf[0])
    half = nb // 2
    pause = 2 * half - half // 4
    lax.fori_loop(0, half, attend(0), 0)
    lax.fori_loop(half, pause, attend(1), 0)
    z0 = combine(0)
    if pause < 2 * half:
        lax.fori_loop(pause, 2 * half, attend(1), 0)

    regroup_h[...] = regroup(GROUP, zn)
    received(zc)
    pieces = nn(regroup(groups, zn), cz[...].reshape(zn * groups * 2, LANES))
    cg[...] = pieces.astype(BF16).reshape(groups, tb, LANES)
    my_group = div(ctx, per_group)
    c2 = {}
    for i in range(1, nb):
        py, px = plus(i)
        there = div((py * zn + z) * xn + px, per_group)
        c2[i] = rcopy(cg.at[there], call.at[b], c2_s.at[i], c2_r.at[i], at(py, z, px))
        c2[i].start()
    call[pl.ds(b, 1)] = cg[pl.ds(my_group, 1)]

    h0 = settle(0, z0)
    sent(*zq, zc)
    z1 = combine(1)
    received(za)
    turn_adapter(0)
    g0 = spread(0, h0)

    sel = iota((rows, rows), 1) == row_of(iota((rows, 1), 0), sizes)
    wanted = jnp.sum(
        jnp.where(sel, jnp.broadcast_to(src_ref[...].astype(F32), (rows, rows)), 0.0),
        axis=1, keepdims=True,
    )
    pick = (wanted == row_of(iota((1, rows), 1), sizes).astype(F32)).astype(F32)
    received(c2)
    cot_rows = nn(pick.T.astype(BF16), call[...].reshape(rows, LANES))
    cot_t[...] = cot_rows.T
    token = iota((nb * 2, 1), 0)
    block = div(token, 2)
    token = 2 * ((div(block, xn) * zn + z) * xn + mod(block, xn)) + mod(token, 2)
    wanted = jnp.sum(
        jnp.where(iota((nb * 2, rows), 1) == token, src_ref[...].astype(F32), 0.0), axis=1, keepdims=True
    )
    pick = (wanted == row_of(iota((1, rows), 1), sizes).astype(F32)).astype(F32)

    h1 = settle(1, z1)
    turn_adapter(1)
    sent(za, z0, z1, c2)
    for j in range(kvl * nb):
        if j % nb:
            q_copy(j, j % nb).wait_send()
            o_copy(j, j % nb).wait_send()
    g1 = spread(1, h1)
    project(0, g0)
    sent(h0, h1, g0)
    project(1, g1)

    for first in range(0, aw, LANES):
        mpre_t[first : first + LANES, :] = mpre[:, first : first + LANES].T
    hx[pl.ds(hd, 1), 0:cpd, 0:rows] = mpre_t[own_ad, :][None]
    power = jnp.sum(squares[...].T, axis=0, keepdims=True)
    hx[pl.ds(hd, 1), cpd : cpd + 8, 0:rows] = jnp.broadcast_to(power, (8, rows))[None]
    one_hot = pick.astype(BF16)
    chosen = functools.reduce(jnp.add, [nn(one_hot, term) for term in split3(mpre[...])])
    base = cpd + 8
    for j in range(aw // LANES):
        hx[pl.ds(hd, 1), base + j * 2 * nb : base + (j + 1) * 2 * nb, :] = chosen[
            :, j * LANES : (j + 1) * LANES
        ][None]
    hxc = {}
    for e in range(1, heads):
        hxc[e] = rcopy(hx.at[hd], hx.at[hd], hx_s.at[e], hx_r.at[e], (ctx, mod(hd + e, heads)))
        hxc[e].start()
    sent(g1)
    received(hxc)
    summed = hx[0]
    for e in range(1, heads):
        summed = summed + hx[e]
    scale = lax.rsqrt(summed[cpd : cpd + 1, 0:rows] / eps_div + 1e-05)

    token_scale = jnp.sum(pick * scale, axis=1, keepdims=True)
    for j in range(aw // LANES):
        pre = token_scale * summed[base + j * 2 * nb : base + (j + 1) * 2 * nb, :]
        out = pre / (1.0 + jnp.exp(-pre))
        for d in range(nb):
            st1s[d, 0:2, j * LANES : (j + 1) * LANES] = out[2 * d : 2 * d + 2, :]
    s1 = {}
    for i in range(1, nb):
        py, px = plus(i)
        s1[i] = rcopy(st1s.at[py * xn + px], st1r.at[b], s1_s.at[i], s1_r.at[i], at(py, z, px))
        s1[i].start()
    st1r[pl.ds(b, 1)] = st1s[pl.ds(b, 1)]
    sent(hxc)

    pre = scale * summed[0:cpd, 0:rows]
    sig = 1.0 / (1.0 + jnp.exp(-pre))
    own = pl.multiple_of(mod(ctx, per_group) * cpd, cpd)
    slope = (cot_t[pl.ds(own, cpd), :] * sig * (1.0 + pre * (1.0 - sig)) * scale).astype(BF16)
    grad_ref[...] = nn(slope, gall[...]) * (rows ** -0.5)

    sent(s1)
    received(s1)
    for py in range(yn):
        tile = st1r[py * xn]
        for px in range(1, xn):
            tile = tile + st1r[py * xn + px]
        stu_ref[:, py * aw : (py + 1) * aw] = tile[0:2, :]


def local(sizes, heads, queries, keys, values, norm_gain, adapter, source_row, cotangent):
    yn, zn, xn = sizes
    nb = yn * xn
    tb = 2 * zn
    rows = nb * tb
    positions, kvw = keys.shape
    kvl = kvw // HD
    nh = kvl * GROUP
    nf = nh * HD
    kr = GROUP * 2
    cpd = adapter.shape[0]
    aw = zn * xn * cpd
    groups = cotangent.shape[1] // LANES
    vm = pltpu.VMEM
    dma = pltpu.SemaphoreType.DMA
    scratch = [
        vm(queries.shape, BF16),
        vm((nh, HD), BF16),
        vm((1, rows), jnp.int32),
        vm(cotangent.shape, BF16),
        vm((positions, kvw), BF16),
        vm((kvl, HD, positions), BF16),
        vm((kvl, positions, 2 * HD), BF16),
        vm((kvl * nb, zn, kr, HD), BF16),
        vm((kvl * nb, zn + 1, kr, HD), BF16),
        vm((kvl * nb, zn + 1, kr, HD), BF16),
        vm((kvl, zn, 2 * kr, HD), BF16),
        vm((kvl, zn, 2 * kr, HD), BF16),
        vm((kvl, zn, kr, HD), BF16),
        vm((kvl, nb, tb, GROUP * HD), BF16),
        vm((rows, nf), BF16),
        vm((rows, aw), F32),
        vm((rows, HD), F32),
        vm((heads, cpd + 8 + 2 * nb * (aw // LANES), max(rows, LANES)), F32),
        vm((zn * kr, positions), F32),
        vm((zn * kr, positions), F32),
        vm((zn * kr, zn * kr), BF16),
        vm((zn, groups * 2, LANES), BF16),
        vm((groups, tb, LANES), BF16),
        vm((nb, tb, LANES), BF16),
        vm((LANES, rows), F32),
        vm((aw, rows), F32),
        vm((nb, 8, aw), F32),
        vm((nb, 8, aw), F32),
        vm((aw, nf), BF16),
        vm((nf, aw), BF16),
        dma((6 + kvl,)),
        dma((kvl * zn,)), dma((kvl * zn,)), dma((kvl * nb,)), dma((kvl * nb,)),
        dma((zn,)), dma((zn,)), dma((nb,)), dma((nb,)),
        dma((kvl * nb,)), dma((kvl * nb,)),
        dma((kvl * zn,)), dma((kvl * zn,)), dma((kvl * zn,)), dma((kvl * zn,)),
        dma((kvl * nb,)), dma((kvl * nb,)),
        dma((heads,)), dma((heads,)),
        dma((nb,)), dma((nb,)), dma((zn,)), dma((zn,)),
    ]
    vmem = pl.BlockSpec(memory_space=pltpu.VMEM)
    hbm = pl.BlockSpec(memory_space=pltpu.HBM)
    return pl.pallas_call(
        functools.partial(kernel, sizes, heads, float(heads * nf)),
        out_shape=(
            jax.ShapeDtypeStruct(cotangent.shape, F32),
            jax.ShapeDtypeStruct(adapter.shape, F32),
        ),
        in_specs=[hbm] * 7,
        out_specs=(vmem, vmem),
        scratch_shapes=scratch,
        compiler_params=pltpu.CompilerParams(
            collective_id=0, has_side_effects=True, vmem_limit_bytes=63 * 1024 * 1024
        ),
        cost_estimate=pl.CostEstimate(
            flops=4 * rows * nh * HD * positions,
            bytes_accessed=4 * positions * kvw,
            transcendentals=rows * nh * positions,
        ),
        name="distill",
    )(queries, keys, values, norm_gain.reshape(nh, HD), adapter, source_row.reshape(1, -1), cotangent)


def solution(mesh, sizes=(YN, ZN, XN)):
    return jax.shard_map(
        functools.partial(local, sizes, mesh.shape["head"]),
        mesh=mesh,
        in_specs=(
            P("ctx", "head"),
            P("ctx", "head"),
            P("ctx", "head"),
            P("head"),
            P("ctx", "head"),
            P(),
            P("ctx", None),
        ),
        out_specs=(P("ctx", None), P("ctx", "head")),
        check_vma=False,
    )
```

time: 2300 us -> 63.2 us (0.03)
  the two profiles are of different devices: /device:TPU:0 before, /device:TPU:1 now
where the time goes in v1:
time: 63.2 us; the launch traced here: 63 us
  Pallas kernels  59.5 us (94%)
  local copies, waits for them, and re-layouts  2.86 us (5%)
  between operations  0.64 us (1%)
    pallas_call x1, Pallas kernels, local(): pl.pallas_call(functools.partial(kernel, sizes, heads, float(heads * nf))...  59.5 us
    unnamed x2, local copies, waits for them, and re-layouts  2.86 us

profile of v1, /device:TPU:1, one launch (start us, length us, event | category | flops | bytes accessed | tf_op | source)
XLA Modules:
  0.0 63.0 jit_solution(6769547525493931788)
XLA Ops:
  0.6 59.5 %distill.1 = (f32[2,1024]{1,0:T(2,128)}, f32[16,2048]{1,0:T(8,128)}) custom-call(bf16[2,2048]{1,0:T(2,128)(2,1)} %q_hbm.1, bf16[2048,256]{1,0:T(8,128)(2,1)} %k_hbm.1, bf16[2048,256]{1,0:T(8,128)(2,1)} %v_hbm.1, bf16[16,128]{1,0:T(8,128)(2,1)} %bitcast.2, bf16[16,2048]{1,0:T(8,128)(2,1)} %ad_hbm.1, s32[1,128]{1,0:T(1,128)} %bitcast.3, bf16[2,1024]{1,0:T(2,128)(2,1)} %cot_hbm.1), custom_call_target="tpu_custom_call" | custom-call | flops 2147483648 | bytes 2097152 | tf_op jit(solution)/shard_map/distill/pallas_call | solution.py:519
  60.2 1.3 %copy.11 = f32[2,1024]{1,0:T(2,128)} copy(f32[2,1024]{1,0:T(2,128)} %get-tuple-element.4) | data formatting | bytes 16384
  61.5 1.6 %copy.12 = f32[16,2048]{1,0:T(8,128)} copy(f32[16,2048]{1,0:T(8,128)} %get-tuple-element.5) | data formatting | bytes 262144

commit v2 on v1

--- a/solution.py
+++ b/solution.py
@@ -128,6 +128,16 @@
         )
 
     q_load = pltpu.make_async_copy(q_hbm, q_ref, loc_sem.at[0])
+    q_load.start()
+    barrier = pltpu.get_barrier_semaphore()
+    partners = (
+        [z_dev(d) for d in range(1, zn)]
+        + [plus_dev(i) for i in range(1, nb)]
+        + [(ctx, mod(hd + e, heads)) for e in range(1, heads)]
+    )
+    for dev in partners:
+        pl.semaphore_signal(barrier, inc=1, device_id=dev, device_id_type=MESH)
+
     cot_load = pltpu.make_async_copy(cot_hbm, cot_ref, loc_sem.at[1])
     k_load = pltpu.make_async_copy(k_hbm, kbuf, loc_sem.at[2])
     own_ad = pl.ds(pl.multiple_of((z * xn + x) * cpd, cpd), cpd)
@@ -142,17 +152,8 @@
                 v_hbm.at[:, k * HD : (k + 1) * HD], vaug.at[k, :, 0:HD], loc_sem.at[6 + k]
             )
         )
-    for load in [q_load, cot_load, k_load, ad_load] + late_loads:
+    for load in [cot_load, k_load, ad_load] + late_loads:
         load.start()
-
-    barrier = pltpu.get_barrier_semaphore()
-    partners = (
-        [z_dev(d) for d in range(1, zn)]
-        + [plus_dev(i) for i in range(1, nb)]
-        + [(ctx, mod(hd + e, heads)) for e in range(1, heads)]
-    )
-    for dev in partners:
-        pl.semaphore_signal(barrier, inc=1, device_id=dev, device_id_type=MESH)
 
     q_load.wait()
     qf = q_ref[...].astype(F32)
@@ -230,43 +231,63 @@
         wide = tile.astype(F32)
         return wide[0:1, :] + wide[1:2, :] + wide[2:3, :]
 
-    def score(j, buf):
-        buf[...] = nn(qall[j].reshape(qrows, HD), k_t[div(j, nb)])
-
-    def weigh(j, k, buf):
-        m = jnp.max(buf[...], axis=1, keepdims=True)
-        p = jnp.exp2((buf[...] - m) * factor).astype(BF16)
+    def score(k, i, count, buf):
+        q = qall[pl.ds(k * nb + i, count)].reshape(count * qrows, HD)
+        buf[0 : count * qrows, :] = nn(q, k_t[k])
+
+    def weigh(k, i, count, buf):
+        s = buf[0 : count * qrows, :]
+        m = jnp.max(s, axis=1, keepdims=True)
+        p = jnp.exp2((buf[0 : count * qrows, :] - m) * factor).astype(BF16)
         oa = nn(p, vaug[k])
         total = oa[:, HD : 2 * HD]
-        o = oa[:, 0:HD] / total
-        osend[j, 0:zn] = o.astype(BF16).reshape(zn, kr, HD)
+        o = (oa[:, 0:HD] / total).astype(BF16)
         lse = m * factor + jnp.log2(total)
-        osend[j, zn] = stat_tile(jnp.sum(jnp.where(eye, lse, 0.0), axis=0, keepdims=True))
+        for c in range(count):
+            part = slice(c * qrows, (c + 1) * qrows)
+            osend[k * nb + i + c, 0:zn] = o[part].reshape(zn, kr, HD)
+            row = jnp.sum(jnp.where(eye, lse[part], 0.0), axis=0, keepdims=True)
+            osend[k * nb + i + c, zn] = stat_tile(row)
+            if i + c > 0:
+                o_copy(k * nb + i + c, i + c).start()
 
     def o_copy(j, i):
         return rcopy(osend.at[j], orecv.at[j], o_s.at[j], o_r.at[j], minus_dev(i))
 
-    def attend(k):
-        def body(t, carry):
-            first, second, third = 2 * t, 2 * t + 1, jnp.minimum(2 * t + 2, kvl * nb - 1)
-            q_copy(second, mod(second, nb)).wait_recv()
-            score(second, sbuf[1])
-            weigh(first, k, sbuf[0])
-
-            @pl.when(mod(first, nb) > 0)
-            def _():
-                o_copy(first, mod(first, nb)).start()
-
-            @pl.when(mod(2 * t + 2, nb) > 0)
-            def _():
-                q_copy(third, mod(third, nb)).wait_recv()
-
-            score(third, sbuf[0])
-            weigh(second, k, sbuf[1])
-            o_copy(second, mod(second, nb)).start()
-            return carry
-
-        return body
+    units = [(1, 1)] + [(i, 2) for i in range(2, nb, 2)]
+
+    def queries_here(k, i, count):
+        for c in range(count):
+            q_copy(k * nb + i + c, i + c).wait_recv()
+
+    def attend(k, carry):
+        for n, (i, count) in enumerate(units):
+            here, there = sbuf[n % 2], sbuf[(n + 1) % 2]
+            if n + 1 < len(units):
+                queries_here(k, *units[n + 1])
+                score(k, *units[n + 1], there)
+                weigh(k, i, count, here)
+            else:
+
+                @pl.when(k == 1)
+                def _():
+                    combine(0)
+
+                later = jnp.minimum(k + 1, kvl - 1)
+
+                @pl.when(k + 1 < kvl)
+                def _():
+                    queries_here(later, *units[0])
+
+                score(later, *units[0], there)
+                weigh(k, i, count, here)
+        return carry
+
+    def z_copies(k):
+        return {
+            d: rcopy(zsend.at[k, z_plus(d)], zrecv.at[k, d], zr_s.at[k * zn + d], zr_r.at[k * zn + d], z_dev(d))
+            for d in ring
+        }
 
     def combine(k):
         for i in range(1, nb):
@@ -285,11 +306,8 @@
         tile = stat_tile(top + jnp.log2(weight_sum))
         for d in range(zn):
             zsend[k, d, kr : 2 * kr, :] = tile
-        return z_group(
-            lambda d: rcopy(
-                zsend.at[k, z_plus(d)], zrecv.at[k, d], zr_s.at[k * zn + d], zr_r.at[k * zn + d], z_dev(d)
-            )
-        )
+        for copy in z_copies(k).values():
+            copy.start()
 
     mine = iota((kr, LANES), 1) == iota((kr, LANES), 0) + z * kr
 
@@ -349,14 +367,13 @@
                     adp[first : first + LANES, h * HD : (h + 1) * HD].astype(F32).T.astype(BF16)
                 )
 
-    score(0, sbuf[0])
-    half = nb // 2
-    pause = 2 * half - half // 4
-    lax.fori_loop(0, half, attend(0), 0)
-    lax.fori_loop(half, pause, attend(1), 0)
-    z0 = combine(0)
-    if pause < 2 * half:
-        lax.fori_loop(pause, 2 * half, attend(1), 0)
+    score(0, 0, 1, sbuf[0])
+    score(1, 0, 1, sbuf[1])
+    weigh(0, 0, 1, sbuf[0])
+    queries_here(0, *units[0])
+    score(0, *units[0], sbuf[0])
+    weigh(1, 0, 1, sbuf[1])
+    lax.fori_loop(0, kvl, attend, 0)
 
     regroup_h[...] = regroup(GROUP, zn)
     received(zc)
@@ -371,9 +388,9 @@
         c2[i].start()
     call[pl.ds(b, 1)] = cg[pl.ds(my_group, 1)]
 
-    h0 = settle(0, z0)
+    h0 = settle(0, z_copies(0))
     sent(*zq, zc)
-    z1 = combine(1)
+    combine(1)
     received(za)
     turn_adapter(0)
     g0 = spread(0, h0)
@@ -395,9 +412,9 @@
     )
     pick = (wanted == row_of(iota((1, rows), 1), sizes).astype(F32)).astype(F32)
 
-    h1 = settle(1, z1)
+    h1 = settle(1, z_copies(1))
     turn_adapter(1)
-    sent(za, z0, z1, c2)
+    sent(za, z_copies(0), z_copies(1), c2)
     for j in range(kvl * nb):
         if j % nb:
             q_copy(j, j % nb).wait_send()
@@ -493,8 +510,8 @@
         vm((rows, aw), F32),
         vm((rows, HD), F32),
         vm((heads, cpd + 8 + 2 * nb * (aw // LANES), max(rows, LANES)), F32),
-        vm((zn * kr, positions), F32),
-        vm((zn * kr, positions), F32),
+        vm((2 * zn * kr, positions), F32),
+        vm((2 * zn * kr, positions), F32),
         vm((zn * kr, zn * kr), BF16),
         vm((zn, groups * 2, LANES), BF16),
         vm((groups, tb, LANES), BF16),
@@ -516,7 +533,7 @@
     ]
     vmem = pl.BlockSpec(memory_space=pltpu.VMEM)
     hbm = pl.BlockSpec(memory_space=pltpu.HBM)
-    return pl.pallas_call(
+    outs = pl.pallas_call(
         functools.partial(kernel, sizes, heads, float(heads * nf)),
         out_shape=(
             jax.ShapeDtypeStruct(cotangent.shape, F32),
@@ -535,6 +552,26 @@
         ),
         name="distill",
     )(queries, keys, values, norm_gain.reshape(nh, HD), adapter, source_row.reshape(1, -1), cotangent)
+    return pl.pallas_call(
+        copy_kernel,
+        out_shape=tuple(jax.ShapeDtypeStruct(out.shape, F32) for out in outs),
+        in_specs=[hbm] * 2,
+        out_specs=(hbm, hbm),
+        scratch_shapes=[dma((2,))],
+        compiler_params=pltpu.CompilerParams(vmem_limit_bytes=63 * 1024 * 1024),
+        name="hand_out",
+    )(*outs)
+
+
+def copy_kernel(a_ref, b_ref, a_out, b_out, sem):
+    copies = [
+        pltpu.make_async_copy(b_ref, b_out, sem.at[0]),
+        pltpu.make_async_copy(a_ref, a_out, sem.at[1]),
+    ]
+    for copy in copies:
+        copy.start()
+    for copy in copies:
+        copy.wait()
 
 
 def solution(mesh, sizes=(YN, ZN, XN)):

time: 63.2 us -> 65.2 us (1.032)
  Pallas kernels: 59.5 us -> 64.4 us
  local copies, waits for them, and re-layouts: 2.86 us -> 0 us
    pallas_call x0 -> x1, Pallas kernels: none -> 5.34 us  [local(): pl.pallas_call(copy_kernel, out_shape=tuple((jax.ShapeDtypeStruct(out.sha...]
    unnamed x2 -> x0, local copies, waits for them, and re-layouts: 2.86 us -> none
where the time goes in v2:
time: 65.2 us; the launch traced here: 65.1 us
  Pallas kernels  64.4 us (99%)
    pallas_call x1, Pallas kernels, local(): pl.pallas_call(functools.partial(kernel, sizes, heads, float(heads * nf))...  59.1 us
    pallas_call x1, Pallas kernels, local(): pl.pallas_call(copy_kernel, out_shape=tuple((jax.ShapeDtypeStruct(out.sha...  5.34 us

profile of v2, /device:TPU:1, one launch (start us, length us, event | category | flops | bytes accessed | tf_op | source)
XLA Modules:
  0.0 65.1 jit_solution(11333838265378293238)
XLA Ops:
  0.6 59.1 %distill.1 = (f32[2,1024]{1,0:T(2,128)}, f32[16,2048]{1,0:T(8,128)}) custom-call(bf16[2,2048]{1,0:T(2,128)(2,1)} %q_hbm.1, bf16[2048,256]{1,0:T(8,128)(2,1)} %k_hbm.1, bf16[2048,256]{1,0:T(8,128)(2,1)} %v_hbm.1, bf16[16,128]{1,0:T(8,128)(2,1)} %bitcast.2, bf16[16,2048]{1,0:T(8,128)(2,1)} %ad_hbm.1, s32[1,128]{1,0:T(1,128)} %bitcast.3, bf16[2,1024]{1,0:T(2,128)(2,1)} %cot_hbm.1), custom_call_target="tpu_custom_call" | custom-call | flops 2147483648 | bytes 2097152 | tf_op jit(solution)/shard_map/distill/pallas_call | solution.py:536
  59.7 5.3 %hand_out.1 = (f32[2,1024]{1,0:T(2,128)}, f32[16,2048]{1,0:T(8,128)}) custom-call(f32[2,1024]{1,0:T(2,128)} %get-tuple-element.4.a_ref, f32[16,2048]{1,0:T(8,128)} %get-tuple-element.5.b_ref), custom_call_target="tpu_custom_call" | custom-call | tf_op jit(solution)/shard_map/hand_out/pallas_call | solution.py:555

commit v3 on v2

--- a/solution.py
+++ b/solution.py
@@ -531,19 +531,20 @@
         dma((heads,)), dma((heads,)),
         dma((nb,)), dma((nb,)), dma((zn,)), dma((zn,)),
     ]
+    args = (queries, keys, values, norm_gain.reshape(nh, HD), adapter, source_row.reshape(1, -1), cotangent)
     vmem = pl.BlockSpec(memory_space=pltpu.VMEM)
     hbm = pl.BlockSpec(memory_space=pltpu.HBM)
-    outs = pl.pallas_call(
+    return pl.pallas_call(
         functools.partial(kernel, sizes, heads, float(heads * nf)),
         out_shape=(
-            jax.ShapeDtypeStruct(cotangent.shape, F32),
-            jax.ShapeDtypeStruct(adapter.shape, F32),
+            pltpu.VMEM(cotangent.shape, F32),
+            pltpu.VMEM(adapter.shape, F32),
         ),
         in_specs=[hbm] * 7,
         out_specs=(vmem, vmem),
         scratch_shapes=scratch,
         compiler_params=pltpu.CompilerParams(
-            collective_id=0, has_side_effects=True, vmem_limit_bytes=63 * 1024 * 1024
+            collective_id=0, has_side_effects=True, vmem_limit_bytes=48 * 1024 * 1024
         ),
         cost_estimate=pl.CostEstimate(
             flops=4 * rows * nh * HD * positions,
@@ -551,27 +552,7 @@
             transcendentals=rows * nh * positions,
         ),
         name="distill",
-    )(queries, keys, values, norm_gain.reshape(nh, HD), adapter, source_row.reshape(1, -1), cotangent)
-    return pl.pallas_call(
-        copy_kernel,
-        out_shape=tuple(jax.ShapeDtypeStruct(out.shape, F32) for out in outs),
-        in_specs=[hbm] * 2,
-        out_specs=(hbm, hbm),
-        scratch_shapes=[dma((2,))],
-        compiler_params=pltpu.CompilerParams(vmem_limit_bytes=63 * 1024 * 1024),
-        name="hand_out",
-    )(*outs)
-
-
-def copy_kernel(a_ref, b_ref, a_out, b_out, sem):
-    copies = [
-        pltpu.make_async_copy(b_ref, b_out, sem.at[0]),
-        pltpu.make_async_copy(a_ref, a_out, sem.at[1]),
-    ]
-    for copy in copies:
-        copy.start()
-    for copy in copies:
-        copy.wait()
+    )(*(pltpu.with_memory_space_constraint(arg, pltpu.HBM) for arg in args))
 
 
 def solution(mesh, sizes=(YN, ZN, XN)):

time: 65.2 us -> 60.5 us (0.928)
  Pallas kernels: 64.4 us -> 58.5 us
  local copies, waits for them, and re-layouts: 0 us -> 1.26 us
    pallas_call x1 -> x0, Pallas kernels: 5.34 us -> none  [local(): pl.pallas_call(copy_kernel, out_shape=tuple((jax.ShapeDtypeStruct(out.sha...]
    unnamed x0 -> x2, local copies, waits for them, and re-layouts: none -> 1.26 us
where the time goes in v3:
time: 60.5 us; the launch traced here: 60.4 us
  Pallas kernels  58.5 us (97%)
  local copies, waits for them, and re-layouts  1.26 us (2%)
  between operations  0.64 us (1%)
    pallas_call x1, Pallas kernels, local(): pl.pallas_call(functools.partial(kernel, sizes, heads, float(heads * nf))...  58.5 us
    unnamed x2, local copies, waits for them, and re-layouts  1.26 us

profile of v3, /device:TPU:1, one launch (start us, length us, event | category | flops | bytes accessed | tf_op | source)
XLA Modules:
  0.0 60.4 jit_solution(9993352332279392916)
XLA Ops:
  0.6 58.5 %distill.1 = (f32[2,1024]{1,0:T(2,128)S(1)}, f32[16,2048]{1,0:T(8,128)S(1)}) custom-call(bf16[2,2048]{1,0:T(2,128)(2,1)} %q_hbm.1, bf16[2048,256]{1,0:T(8,128)(2,1)} %k_hbm.1, bf16[2048,256]{1,0:T(8,128)(2,1)} %v_hbm.1, bf16[16,128]{1,0:T(8,128)(2,1)} %bitcast.2, bf16[16,2048]{1,0:T(8,128)(2,1)} %ad_hbm.1, s32[1,128]{1,0:T(1,128)} %bitcast.3, ...), custom_call_target="tpu_custom_call" | custom-call | flops 2147483648 | bytes 2097152 | tf_op jit(solution)/shard_map/distill/pallas_call | solution.py:537
  59.2 0.6 copy.11
  59.8 0.7 %copy.12 = f32[16,2048]{1,0:T(8,128)} copy(f32[16,2048]{1,0:T(8,128)S(1)} %get-tuple-element.3) | data formatting | bytes 262144

commit v4 on v3

--- a/solution.py
+++ b/solution.py
@@ -59,7 +59,7 @@
 def kernel(sizes, heads, eps_div, q_hbm, k_hbm, v_hbm, gain_hbm, ad_hbm, src_hbm, cot_hbm,
            stu_ref, grad_ref,
            q_ref, gain_ref, src_ref, cot_ref, kbuf, k_t, vaug, qall, osend, orecv, zsend, zrecv,
-           hz, hall, gall, mpre, squares, hx, s_even, s_odd, regroup_h, cz, cg, call, cot_t, mpre_t, st1s, st1r,
+           hz, hall, gall, mpre, squares, hx, s_even, s_odd, shares, regroup_h, cz, cg, call, cot_t, mpre_t, st1s, st1r,
            adp, ad_t,
            loc_sem, zq_s, zq_r, q2_s, q2_r, zc_s, zc_r, c2_s, c2_r, o_s, o_r,
            zr_s, zr_r, hz_s, hz_r, h2_s, h2_r, hx_s, hx_r, s1_s, s1_r, za_s, za_r):
@@ -89,7 +89,15 @@
     def z_plus(d):
         return mod(z + d, zn)
 
-    ring = sorted(range(1, zn), key=lambda d: -min(d, zn - d))
+    def loop(first, last, body):
+        def step(n, carry):
+            body(n)
+            return carry
+
+        lax.fori_loop(first, last, step, 0)
+
+    def over_ring(body):
+        loop(0, zn - 1, lambda n: body(zn // 2 + jnp.where(mod(n, 2) == 1, -div(n + 1, 2), div(n, 2))))
 
     def z_dev(d):
         return at(y, z_plus(d), x)
@@ -130,13 +138,13 @@
     q_load = pltpu.make_async_copy(q_hbm, q_ref, loc_sem.at[0])
     q_load.start()
     barrier = pltpu.get_barrier_semaphore()
-    partners = (
-        [z_dev(d) for d in range(1, zn)]
-        + [plus_dev(i) for i in range(1, nb)]
-        + [(ctx, mod(hd + e, heads)) for e in range(1, heads)]
-    )
-    for dev in partners:
+
+    def greet(dev):
         pl.semaphore_signal(barrier, inc=1, device_id=dev, device_id_type=MESH)
+
+    over_ring(lambda d: greet(z_dev(d)))
+    loop(1, nb, lambda i: greet(plus_dev(i)))
+    loop(1, heads, lambda e: greet((ctx, mod(hd + e, heads))))
 
     cot_load = pltpu.make_async_copy(cot_hbm, cot_ref, loc_sem.at[1])
     k_load = pltpu.make_async_copy(k_hbm, kbuf, loc_sem.at[2])
@@ -166,36 +174,47 @@
     cz[pl.ds(z, 1)] = jnp.concatenate(
         [cf[:, g * LANES : (g + 1) * LANES] for g in range(groups)], axis=0
     ).astype(BF16)[None]
-    pl.semaphore_wait(barrier, len(partners))
+    pl.semaphore_wait(barrier, zn - 1 + nb - 1 + heads - 1)
+
+    class Copies:
+        def __init__(self, over, make):
+            self.over, self.make = over, make
+
+        def start(self):
+            self.over(lambda n: self.make(n).start())
+            return self
 
     def z_group(make):
-        copies = {d: make(d) for d in ring}
-        for copy in copies.values():
-            copy.start()
-        return copies
+        return Copies(over_ring, make)
+
+    def plane_group(make):
+        return Copies(lambda body: loop(1, nb, body), make)
 
     def received(copies):
-        for copy in copies.values():
-            copy.wait_recv()
+        copies.over(lambda n: copies.make(n).wait_recv())
 
     def sent(*groups_of_copies):
         for copies in groups_of_copies:
-            for copy in copies.values():
-                copy.wait_send()
+            copies.over(lambda n, copies=copies: copies.make(n).wait_send())
 
     zq = [
         z_group(
             lambda d, k=k: rcopy(
                 qall.at[k * nb, z], qall.at[k * nb, z], zq_s.at[k * zn + d], zq_r.at[k * zn + d], z_dev(d)
             )
-        )
+        ).start()
         for k in range(kvl)
     ]
-    zc = z_group(lambda d: rcopy(cz.at[z], cz.at[z], zc_s.at[d], zc_r.at[d], z_dev(d)))
+    zc = z_group(lambda d: rcopy(cz.at[z], cz.at[z], zc_s.at[d], zc_r.at[d], z_dev(d))).start()
 
     k_load.wait()
-    for k in range(kvl):
-        k_t[k] = kbuf[:, k * HD : (k + 1) * HD].astype(F32).T.astype(BF16)
+
+    def turn_keys(c):
+        lines = pl.ds(pl.multiple_of(c * LANES, LANES), LANES)
+        for k in range(kvl):
+            k_t[k, :, lines] = kbuf[lines, k * HD : (k + 1) * HD].astype(F32).T.astype(BF16)
+
+    loop(0, kbuf.shape[0] // LANES, turn_keys)
     for k in range(kvl):
         vaug[k, :, HD : 2 * HD] = jnp.ones((vaug.shape[1], HD), BF16)
 
@@ -204,16 +223,18 @@
 
     for k in range(kvl):
         received(zq[k])
-        for i in range(1, nb):
-            q_copy(k * nb + i, i).start()
-
-    for d in range(zn):
+        loop(1, nb, lambda i, k=k: q_copy(k * nb + i, i).start())
+
+
+    def blank(d):
         for e in range(1, xn):
             other = pl.multiple_of((d * xn + mod(x + e, xn)) * cpd, cpd)
             adp[pl.ds(other, cpd), :] = jnp.zeros((cpd, nh * HD), BF16)
+
+    loop(0, zn, blank)
     st1s[...] = jnp.zeros_like(st1s)
     ad_load.wait()
-    za = z_group(lambda d: rcopy(adp.at[own_ad], adp.at[own_ad], za_s.at[d], za_r.at[d], z_dev(d)))
+    za = z_group(lambda d: rcopy(adp.at[own_ad], adp.at[own_ad], za_s.at[d], za_r.at[d], z_dev(d))).start()
     for load in late_loads:
         load.wait()
 
@@ -231,83 +252,84 @@
         wide = tile.astype(F32)
         return wide[0:1, :] + wide[1:2, :] + wide[2:3, :]
 
-    def score(k, i, count, buf):
-        q = qall[pl.ds(k * nb + i, count)].reshape(count * qrows, HD)
-        buf[0 : count * qrows, :] = nn(q, k_t[k])
-
-    def weigh(k, i, count, buf):
-        s = buf[0 : count * qrows, :]
-        m = jnp.max(s, axis=1, keepdims=True)
-        p = jnp.exp2((buf[0 : count * qrows, :] - m) * factor).astype(BF16)
+    def unit(n):
+        k = jnp.where(n < kvl, n, jnp.where(n < kvl + nb - 1, 0, 1))
+        i = jnp.where(n < kvl, 0, jnp.where(n < kvl + nb - 1, n - kvl + 1, n - kvl - nb + 2))
+        return k, i
+
+    def score(n, buf):
+        k, i = unit(n)
+        buf[...] = nn(qall[k * nb + i].reshape(qrows, HD), k_t[k])
+
+    def weigh(n, buf):
+        k, i = unit(n)
+        j = k * nb + i
+        m = jnp.max(buf[...], axis=1, keepdims=True)
+        p = jnp.exp2((buf[...] - m) * factor).astype(BF16)
         oa = nn(p, vaug[k])
         total = oa[:, HD : 2 * HD]
-        o = (oa[:, 0:HD] / total).astype(BF16)
+        o = oa[:, 0:HD] / total
+        osend[j, 0:zn] = o.astype(BF16).reshape(zn, kr, HD)
         lse = m * factor + jnp.log2(total)
-        for c in range(count):
-            part = slice(c * qrows, (c + 1) * qrows)
-            osend[k * nb + i + c, 0:zn] = o[part].reshape(zn, kr, HD)
-            row = jnp.sum(jnp.where(eye, lse[part], 0.0), axis=0, keepdims=True)
-            osend[k * nb + i + c, zn] = stat_tile(row)
-            if i + c > 0:
-                o_copy(k * nb + i + c, i + c).start()
+        osend[j, zn] = stat_tile(jnp.sum(jnp.where(eye, lse, 0.0), axis=0, keepdims=True))
+
+        @pl.when(i > 0)
+        def _():
+            o_copy(j, i).start()
 
     def o_copy(j, i):
         return rcopy(osend.at[j], orecv.at[j], o_s.at[j], o_r.at[j], minus_dev(i))
 
-    units = [(1, 1)] + [(i, 2) for i in range(2, nb, 2)]
-
-    def queries_here(k, i, count):
-        for c in range(count):
-            q_copy(k * nb + i + c, i + c).wait_recv()
-
-    def attend(k, carry):
-        for n, (i, count) in enumerate(units):
-            here, there = sbuf[n % 2], sbuf[(n + 1) % 2]
-            if n + 1 < len(units):
-                queries_here(k, *units[n + 1])
-                score(k, *units[n + 1], there)
-                weigh(k, i, count, here)
-            else:
-
-                @pl.when(k == 1)
-                def _():
-                    combine(0)
-
-                later = jnp.minimum(k + 1, kvl - 1)
-
-                @pl.when(k + 1 < kvl)
-                def _():
-                    queries_here(later, *units[0])
-
-                score(later, *units[0], there)
-                weigh(k, i, count, here)
-        return carry
+    last = kvl * nb - 1
+
+    def queries_here(n):
+        k, i = unit(jnp.minimum(n, last))
+
+        @pl.when((i > 0) & (n <= last))
+        def _():
+            q_copy(k * nb + i, i).wait_recv()
+
+    def attend(t):
+        queries_here(2 * t + 1)
+        score(2 * t + 1, sbuf[1])
+        weigh(2 * t, sbuf[0])
+
+        @pl.when(2 * t + 2 == last - 1)
+        def _():
+            combine(0)
+
+        queries_here(2 * t + 2)
+        score(jnp.minimum(2 * t + 2, last), sbuf[0])
+        weigh(2 * t + 1, sbuf[1])
 
     def z_copies(k):
-        return {
-            d: rcopy(zsend.at[k, z_plus(d)], zrecv.at[k, d], zr_s.at[k * zn + d], zr_r.at[k * zn + d], z_dev(d))
-            for d in ring
-        }
+        return z_group(
+            lambda d: rcopy(
+                zsend.at[k, z_plus(d)], zrecv.at[k, d], zr_s.at[k * zn + d], zr_r.at[k * zn + d], z_dev(d)
+            )
+        )
 
     def combine(k):
-        for i in range(1, nb):
-            o_copy(k * nb + i, i).wait_recv()
-        parts = [(osend if i == 0 else orecv).at[k * nb + i] for i in range(nb)]
-        stats = [stat_row(part[zn]) for part in parts]
+        loop(1, nb, lambda i: o_copy(k * nb + i, i).wait_recv())
+        orecv[k * nb] = osend[k * nb]
+        stats = [stat_row(orecv[k * nb + i, zn]) for i in range(nb)]
         top = functools.reduce(jnp.maximum, stats)
         weights = [jnp.exp2(st - top) for st in stats]
         weight_sum = functools.reduce(jnp.add, weights)
         inverse = 1.0 / weight_sum
-        acc = jnp.zeros((qrows, HD), F32)
         for i in range(nb):
-            share = jnp.where(eye, weights[i] * inverse, 0.0)[:, 0:qrows].astype(BF16)
-            acc = acc + nn(share, parts[i][0:zn].reshape(qrows, HD))
+            shares[i : i + 1, :] = weights[i] * inverse
+
+        def add(i, acc):
+            share = jnp.where(eye, shares[pl.ds(i, 1), :], 0.0)[:, 0:qrows].astype(BF16)
+            return acc + nn(share, orecv[k * nb + i, 0:zn].reshape(qrows, HD))
+
+        acc = lax.fori_loop(0, nb, add, jnp.zeros((qrows, HD), F32))
         zsend[k, :, 0:kr, :] = acc.astype(BF16).reshape(zn, kr, HD)
         tile = stat_tile(top + jnp.log2(weight_sum))
         for d in range(zn):
             zsend[k, d, kr : 2 * kr, :] = tile
-        for copy in z_copies(k).values():
-            copy.start()
+        z_copies(k).start()
 
     mine = iota((kr, LANES), 1) == iota((kr, LANES), 0) + z * kr
 
@@ -325,67 +347,63 @@
         hz[k, pl.ds(z, 1)] = acc.astype(BF16)[None]
         return z_group(
             lambda d: rcopy(hz.at[k, z], hz.at[k, z], hz_s.at[k * zn + d], hz_r.at[k * zn + d], z_dev(d))
-        )
+        ).start()
 
     def spread(k, copies):
         received(copies)
         pieces = nn(regroup_h[...], hz[k].reshape(zn * kr, HD)).astype(BF16)
         for h in range(GROUP):
             hall[k, pl.ds(b, 1), :, h * HD : (h + 1) * HD] = pieces[h * tb : (h + 1) * tb, :][None]
-        copies = {
-            i: rcopy(hall.at[k, b], hall.at[k, b], h2_s.at[k * nb + i], h2_r.at[k * nb + i], plus_dev(i))
-            for i in range(1, nb)
-        }
-        for copy in copies.values():
-            copy.start()
-        return copies
+        return plane_group(
+            lambda i: rcopy(hall.at[k, b], hall.at[k, b], h2_s.at[k * nb + i], h2_r.at[k * nb + i], plus_dev(i))
+        ).start()
 
     def project(k, copies):
         gain = gain_ref[...].astype(F32)
-        for i in range(nb):
-            if i > 0:
-                copies[i].wait_recv()
+        def gather(i):
+            @pl.when(i > 0)
+            def _():
+                copies.make(i).wait_recv()
+
             my, mx = minus(i)
             there = my * xn + mx
-            hidden = hall[k, there].astype(F32)
             lines = pl.ds(pl.multiple_of(there * tb, tb), tb)
             partial = jnp.zeros((tb, HD), F32)
             for h in range(GROUP):
-                piece = hidden[:, h * HD : (h + 1) * HD]
+                piece = hall[k, there, :, h * HD : (h + 1) * HD].astype(F32)
                 partial = partial + piece * piece
                 head = k * GROUP + h
                 gall[lines, head * HD : (head + 1) * HD] = (piece * gain[head : head + 1, :]).astype(BF16)
             squares[lines, :] = partial if k == 0 else squares[lines, :] + partial
+
+        loop(0, nb, gather)
         width = GROUP * HD
         part = nn(gall[:, k * width : (k + 1) * width], ad_t[k * width : (k + 1) * width, :])
         mpre[...] = part if k == 0 else mpre[...] + part
 
     def turn_adapter(k):
-        for h in range(k * GROUP, (k + 1) * GROUP):
+        def turn(h):
+            lanes = pl.ds(pl.multiple_of(h * HD, HD), HD)
             for first in range(0, aw, LANES):
-                ad_t[h * HD : (h + 1) * HD, first : first + LANES] = (
-                    adp[first : first + LANES, h * HD : (h + 1) * HD].astype(F32).T.astype(BF16)
-                )
-
-    score(0, 0, 1, sbuf[0])
-    score(1, 0, 1, sbuf[1])
-    weigh(0, 0, 1, sbuf[0])
-    queries_here(0, *units[0])
-    score(0, *units[0], sbuf[0])
-    weigh(1, 0, 1, sbuf[1])
-    lax.fori_loop(0, kvl, attend, 0)
+                ad_t[lanes, first : first + LANES] = adp[first : first + LANES, lanes].astype(F32).T.astype(BF16)
+
+        loop(k * GROUP, (k + 1) * GROUP, turn)
+
+    score(0, sbuf[0])
+    loop(0, kvl * nb // 2, attend)
 
     regroup_h[...] = regroup(GROUP, zn)
     received(zc)
     pieces = nn(regroup(groups, zn), cz[...].reshape(zn * groups * 2, LANES))
     cg[...] = pieces.astype(BF16).reshape(groups, tb, LANES)
     my_group = div(ctx, per_group)
-    c2 = {}
-    for i in range(1, nb):
+
+    def c2_copy(i):
         py, px = plus(i)
         there = div((py * zn + z) * xn + px, per_group)
-        c2[i] = rcopy(cg.at[there], call.at[b], c2_s.at[i], c2_r.at[i], at(py, z, px))
-        c2[i].start()
+        return rcopy(cg.at[there], call.at[b], c2_s.at[i], c2_r.at[i], at(py, z, px))
+
+    c2 = plane_group(c2_copy).start()
     call[pl.ds(b, 1)] = cg[pl.ds(my_group, 1)]
 
     h0 = settle(0, z_copies(0))
@@ -415,10 +433,8 @@
     h1 = settle(1, z_copies(1))
     turn_adapter(1)
     sent(za, z_copies(0), z_copies(1), c2)
-    for j in range(kvl * nb):
-        if j % nb:
-            q_copy(j, j % nb).wait_send()
-            o_copy(j, j % nb).wait_send()
+    for k in range(kvl):
+        sent(plane_group(lambda i, k=k: q_copy(k * nb + i, i)), plane_group(lambda i, k=k: o_copy(k * nb + i, i)))
     g1 = spread(1, h1)
     project(0, g0)
     sent(h0, h1, g0)
@@ -436,10 +452,10 @@
         hx[pl.ds(hd, 1), base + j * 2 * nb : base + (j + 1) * 2 * nb, :] = chosen[
             :, j * LANES : (j + 1) * LANES
         ][None]
-    hxc = {}
-    for e in range(1, heads):
-        hxc[e] = rcopy(hx.at[hd], hx.at[hd], hx_s.at[e], hx_r.at[e], (ctx, mod(hd + e, heads)))
-        hxc[e].start()
+    hxc = Copies(
+        lambda body: loop(1, heads, body),
+        lambda e: rcopy(hx.at[hd], hx.at[hd], hx_s.at[e], hx_r.at[e], (ctx, mod(hd + e, heads))),
+    ).start()
     sent(g1)
     received(hxc)
     summed = hx[0]
@@ -453,11 +469,12 @@
         out = pre / (1.0 + jnp.exp(-pre))
         for d in range(nb):
             st1s[d, 0:2, j * LANES : (j + 1) * LANES] = out[2 * d : 2 * d + 2, :]
-    s1 = {}
-    for i in range(1, nb):
+
+    def s1_copy(i):
         py, px = plus(i)
-        s1[i] = rcopy(st1s.at[py * xn + px], st1r.at[b], s1_s.at[i], s1_r.at[i], at(py, z, px))
-        s1[i].start()
+        return rcopy(st1s.at[py * xn + px], st1r.at[b], s1_s.at[i], s1_r.at[i], at(py, z, px))
+
+    s1 = plane_group(s1_copy).start()
     st1r[pl.ds(b, 1)] = st1s[pl.ds(b, 1)]
     sent(hxc)
 
@@ -510,8 +527,9 @@
         vm((rows, aw), F32),
         vm((rows, HD), F32),
         vm((heads, cpd + 8 + 2 * nb * (aw // LANES), max(rows, LANES)), F32),
-        vm((2 * zn * kr, positions), F32),
-        vm((2 * zn * kr, positions), F32),
+        vm((zn * kr, positions), F32),
+        vm((zn * kr, positions), F32),
+        vm((nb, LANES), F32),
         vm((zn * kr, zn * kr), BF16),
         vm((zn, groups * 2, LANES), BF16),
         vm((groups, tb, LANES), BF16),

time: 60.5 us -> 62.7 us (1.036)
  Pallas kernels: 58.5 us -> 60.7 us
    pallas_call x1, Pallas kernels: 58.5 us -> 60.7 us  [local(): pl.pallas_call(functools.partial(kernel, sizes, heads, float(heads * nf))...]
where the time goes in v4:
time: 62.7 us; the launch traced here: 62.6 us
  Pallas kernels  60.7 us (97%)
  local copies, waits for them, and re-layouts  1.26 us (2%)
  between operations  0.64 us (1%)
    pallas_call x1, Pallas kernels, local(): pl.pallas_call(functools.partial(kernel, sizes, heads, float(heads * nf))...  60.7 us
    unnamed x2, local copies, waits for them, and re-layouts  1.26 us

profile of v4, /device:TPU:1, one launch (start us, length us, event | category | flops | bytes accessed | tf_op | source)
XLA Modules:
  0.0 62.6 jit_solution(5022708148360635789)
XLA Ops:
  0.6 60.7 %distill.1 = (f32[2,1024]{1,0:T(2,128)S(1)}, f32[16,2048]{1,0:T(8,128)S(1)}) custom-call(bf16[2,2048]{1,0:T(2,128)(2,1)} %q_hbm.1, bf16[2048,256]{1,0:T(8,128)(2,1)} %k_hbm.1, bf16[2048,256]{1,0:T(8,128)(2,1)} %v_hbm.1, bf16[16,128]{1,0:T(8,128)(2,1)} %bitcast.2, bf16[16,2048]{1,0:T(8,128)(2,1)} %ad_hbm.1, s32[1,128]{1,0:T(1,128)} %bitcast.3, ...), custom_call_target="tpu_custom_call" | custom-call | flops 2147483648 | bytes 2097152 | tf_op jit(solution)/shard_map/distill/pallas_call | solution.py:555
  61.3 0.6 copy.11
  61.9 0.7 %copy.12 = f32[16,2048]{1,0:T(8,128)} copy(f32[16,2048]{1,0:T(8,128)S(1)} %get-tuple-element.3) | data formatting | bytes 262144

commit v5 on v3

--- a/solution.py
+++ b/solution.py
@@ -388,12 +388,11 @@
         c2[i].start()
     call[pl.ds(b, 1)] = cg[pl.ds(my_group, 1)]
 
+    combine(1)
+    sent(*zq, zc)
     h0 = settle(0, z_copies(0))
-    sent(*zq, zc)
-    combine(1)
     received(za)
     turn_adapter(0)
-    g0 = spread(0, h0)
 
     sel = iota((rows, rows), 1) == row_of(iota((rows, 1), 0), sizes)
     wanted = jnp.sum(
@@ -413,6 +412,7 @@
     pick = (wanted == row_of(iota((1, rows), 1), sizes).astype(F32)).astype(F32)
 
     h1 = settle(1, z_copies(1))
+    g0 = spread(0, h0)
     turn_adapter(1)
     sent(za, z_copies(0), z_copies(1), c2)
     for j in range(kvl * nb):

time: 60.5 us -> 59.2 us (0.979)
  Pallas kernels: 58.5 us -> 57.1 us
    pallas_call x1, Pallas kernels: 58.5 us -> 57.1 us  [local(): pl.pallas_call(functools.partial(kernel, sizes, heads, float(heads * nf))...]
where the time goes in v5:
time: 59.2 us; the launch traced here: 59 us
  Pallas kernels  57.1 us (96%)
  local copies, waits for them, and re-layouts  1.26 us (2%)
  between operations  0.64 us (1%)
    pallas_call x1, Pallas kernels, local(): pl.pallas_call(functools.partial(kernel, sizes, heads, float(heads * nf))...  57.1 us
    unnamed x2, local copies, waits for them, and re-layouts  1.26 us

profile of v5, /device:TPU:1, one launch (start us, length us, event | category | flops | bytes accessed | tf_op | source)
XLA Modules:
  0.0 59.0 jit_solution(9521389449975396924)
XLA Ops:
  0.6 57.1 %distill.1 = (f32[2,1024]{1,0:T(2,128)S(1)}, f32[16,2048]{1,0:T(8,128)S(1)}) custom-call(bf16[2,2048]{1,0:T(2,128)(2,1)} %q_hbm.1, bf16[2048,256]{1,0:T(8,128)(2,1)} %k_hbm.1, bf16[2048,256]{1,0:T(8,128)(2,1)} %v_hbm.1, bf16[16,128]{1,0:T(8,128)(2,1)} %bitcast.2, bf16[16,2048]{1,0:T(8,128)(2,1)} %ad_hbm.1, s32[1,128]{1,0:T(1,128)} %bitcast.3, ...), custom_call_target="tpu_custom_call" | custom-call | flops 2147483648 | bytes 2097152 | tf_op jit(solution)/shard_map/distill/pallas_call | solution.py:537
  57.8 0.6 %copy.11 = f32[2,1024]{1,0:T(2,128)} copy(f32[2,1024]{1,0:T(2,128)S(1)} %get-tuple-element.2) | data formatting | bytes 16384
  58.4 0.7 %copy.12 = f32[16,2048]{1,0:T(8,128)} copy(f32[16,2048]{1,0:T(8,128)S(1)} %get-tuple-element.3) | data formatting | bytes 262144

commit v6 on v5

--- a/solution.py
+++ b/solution.py
@@ -59,7 +59,7 @@
 def kernel(sizes, heads, eps_div, q_hbm, k_hbm, v_hbm, gain_hbm, ad_hbm, src_hbm, cot_hbm,
            stu_ref, grad_ref,
            q_ref, gain_ref, src_ref, cot_ref, kbuf, k_t, vaug, qall, osend, orecv, zsend, zrecv,
-           hz, hall, gall, mpre, squares, hx, s_even, s_odd, regroup_h, cz, cg, call, cot_t, mpre_t, st1s, st1r,
+           hz, hall, gall, mpre, squares, hx, s_even, s_odd, rowbuf, regroup_h, cz, cg, call, cot_t, mpre_t, st1s, st1r,
            adp, ad_t,
            loc_sem, zq_s, zq_r, q2_s, q2_r, zc_s, zc_r, c2_s, c2_r, o_s, o_r,
            zr_s, zr_r, hz_s, hz_r, h2_s, h2_r, hx_s, hx_r, s1_s, s1_r, za_s, za_r):
@@ -94,24 +94,20 @@
     def z_dev(d):
         return at(y, z_plus(d), x)
 
-    def steps(i):
-        far, turn = div(i, yn), mod(i, yn)
-        if isinstance(i, int):
-            near = (0, 1, 3, 2)[turn] if yn == 4 else turn
-            return (near if far == 0 else (2, 1, 3, 0)[turn] if yn == 4 else yn - 1 - turn), far
-        if yn == 4:
-            first = jnp.where(turn == 2, 3, jnp.where(turn == 3, 2, turn))
-            second = jnp.where(turn == 0, 2, jnp.where(turn == 1, 1, jnp.where(turn == 2, 3, 0)))
-        else:
-            first, second = turn, yn - 1 - turn
-        return jnp.where(far == 0, first, second), far
+    steps = sorted(
+        ((dy, dx) for dy in range(yn) for dx in range(xn)), key=lambda st: (min(st[0], yn - st[0]) + st[1], st[1], st[0])
+    )
+    far_first = range(nb - 1, 0, -1)
+    planes = sorted(range(zn), key=lambda d: (min(d, zn - d), d))
+    near = 1 + 2 * (zn // 4)
+    parts_of = ((0, near), (near, zn))
 
     def plus(i):
-        dy, dx = steps(i)
+        dy, dx = steps[i]
         return mod(y + dy, yn), mod(x + dx, xn)
 
     def minus(i):
-        dy, dx = steps(i)
+        dy, dx = steps[i]
         return mod(y + yn - dy, yn), mod(x + xn - dx, xn)
 
     def plus_dev(i):
@@ -158,9 +154,9 @@
     q_load.wait()
     qf = q_ref[...].astype(F32)
     for k in range(kvl):
-        qall[k * nb, pl.ds(z, 1)] = jnp.concatenate(
+        qall[k * nb, 0] = jnp.concatenate(
             [qf[:, (k * GROUP + h) * HD : (k * GROUP + h + 1) * HD] for h in range(GROUP)], axis=0
-        ).astype(BF16)[None]
+        ).astype(BF16)
     cot_load.wait()
     cf = cot_ref[...].astype(F32)
     cz[pl.ds(z, 1)] = jnp.concatenate(
@@ -183,14 +179,13 @@
             for copy in copies.values():
                 copy.wait_send()
 
-    zq = [
-        z_group(
-            lambda d, k=k: rcopy(
-                qall.at[k * nb, z], qall.at[k * nb, z], zq_s.at[k * zn + d], zq_r.at[k * zn + d], z_dev(d)
-            )
+    def zq_copy(k, d):
+        slot = planes.index((zn - d) % zn)
+        return rcopy(
+            qall.at[k * nb, 0], qall.at[k * nb, slot], zq_s.at[k * zn + d], zq_r.at[k * zn + d], z_dev(d)
         )
-        for k in range(kvl)
-    ]
+
+    zq = [z_group(lambda d, k=k: zq_copy(k, d)) for k in range(kvl)]
     zc = z_group(lambda d: rcopy(cz.at[z], cz.at[z], zc_s.at[d], zc_r.at[d], z_dev(d)))
 
     k_load.wait()
@@ -199,14 +194,20 @@
     for k in range(kvl):
         vaug[k, :, HD : 2 * HD] = jnp.ones((vaug.shape[1], HD), BF16)
 
-    def q_copy(j, i):
-        return rcopy(qall.at[j - i], qall.at[j], q2_s.at[j], q2_r.at[j], plus_dev(i))
-
-    for k in range(kvl):
-        received(zq[k])
-        for i in range(1, nb):
-            q_copy(k * nb + i, i).start()
-
+    def q_copy(part, j, i):
+        lines = slice(*parts_of[part])
+        n = part * kvl * nb + j
+        return rcopy(qall.at[j - i, lines], qall.at[j, lines], q2_s.at[n], q2_r.at[n], plus_dev(i))
+
+    def pass_on(part):
+        for k in range(kvl):
+            for d in planes[slice(*parts_of[part])]:
+                if d:
+                    zq[k][zn - d].wait_recv()
+            for i in range(1, nb):
+                q_copy(part, k * nb + i, i).start()
+
+    pass_on(0)
     for d in range(zn):
         for e in range(1, xn):
             other = pl.multiple_of((d * xn + mod(x + e, xn)) * cpd, cpd)
@@ -220,6 +221,11 @@
     factor = (HD ** -0.5) * LOG2E
     qrows = zn * kr
     eye = iota((qrows, LANES), 0) == iota((qrows, LANES), 1)
+    group_rows = [(last - first) * kr for first, last in parts_of]
+    eyes = [
+        iota((size, LANES), 0) + first * kr == iota((size, LANES), 1)
+        for size, (first, last) in zip(group_rows, parts_of)
+    ]
 
     def stat_tile(row):
         high, middle, low = split3(row)
@@ -231,61 +237,54 @@
         wide = tile.astype(F32)
         return wide[0:1, :] + wide[1:2, :] + wide[2:3, :]
 
-    def score(k, i, count, buf):
-        q = qall[pl.ds(k * nb + i, count)].reshape(count * qrows, HD)
-        buf[0 : count * qrows, :] = nn(q, k_t[k])
-
-    def weigh(k, i, count, buf):
-        s = buf[0 : count * qrows, :]
-        m = jnp.max(s, axis=1, keepdims=True)
-        p = jnp.exp2((buf[0 : count * qrows, :] - m) * factor).astype(BF16)
+    def score(part, k, i, count, buf):
+        size = count * group_rows[part]
+        q = qall[k * nb + i : k * nb + i + count, slice(*parts_of[part])].reshape(size, HD)
+        buf[0:size, :] = nn(q, k_t[k])
+
+    def weigh(part, k, i, count, buf):
+        size = group_rows[part]
+        first, last = parts_of[part]
+        m = jnp.max(buf[0 : count * size, :], axis=1, keepdims=True)
+        p = jnp.exp2((buf[0 : count * size, :] - m) * factor).astype(BF16)
         oa = nn(p, vaug[k])
         total = oa[:, HD : 2 * HD]
         o = (oa[:, 0:HD] / total).astype(BF16)
         lse = m * factor + jnp.log2(total)
         for c in range(count):
-            part = slice(c * qrows, (c + 1) * qrows)
-            osend[k * nb + i + c, 0:zn] = o[part].reshape(zn, kr, HD)
-            row = jnp.sum(jnp.where(eye, lse[part], 0.0), axis=0, keepdims=True)
-            osend[k * nb + i + c, zn] = stat_tile(row)
-            if i + c > 0:
-                o_copy(k * nb + i + c, i + c).start()
+            j = k * nb + i + c
+            lines = slice(c * size, (c + 1) * size)
+            osend[j, first:last] = o[lines].reshape(last - first, kr, HD)
+            row = jnp.sum(jnp.where(eyes[part], lse[lines], 0.0), axis=0, keepdims=True)
+            if part == 0:
+                rowbuf[j : j + 1, :] = row
+            else:
+                osend[j, zn] = stat_tile(rowbuf[j : j + 1, :] + row)
+                if i + c > 0:
+                    o_copy(j, i + c).start()
 
     def o_copy(j, i):
         return rcopy(osend.at[j], orecv.at[j], o_s.at[j], o_r.at[j], minus_dev(i))
 
-    units = [(1, 1)] + [(i, 2) for i in range(2, nb, 2)]
-
-    def queries_here(k, i, count):
-        for c in range(count):
-            q_copy(k * nb + i + c, i + c).wait_recv()
-
-    def attend(k, carry):
-        for n, (i, count) in enumerate(units):
-            here, there = sbuf[n % 2], sbuf[(n + 1) % 2]
+    def attend(units, pause=None):
+        def begin(n):
+            part, k, i, count = units[n]
+            for c in range(count):
+                if i + c > 0:
+                    q_copy(part, k * nb + i + c, i + c).wait_recv()
+            score(*units[n], sbuf[n % 2])
+
+        begin(0)
+        for n, unit in enumerate(units):
+            if n + 1 == pause:
+                combine(0)
             if n + 1 < len(units):
-                queries_here(k, *units[n + 1])
-                score(k, *units[n + 1], there)
-                weigh(k, i, count, here)
-            else:
-
-                @pl.when(k == 1)
-                def _():
-                    combine(0)
-
-                later = jnp.minimum(k + 1, kvl - 1)
-
-                @pl.when(k + 1 < kvl)
-                def _():
-                    queries_here(later, *units[0])
-
-                score(later, *units[0], there)
-                weigh(k, i, count, here)
-        return carry
+                begin(n + 1)
+            weigh(*unit, sbuf[n % 2])
 
     def z_copies(k):
         return {
-            d: rcopy(zsend.at[k, z_plus(d)], zrecv.at[k, d], zr_s.at[k * zn + d], zr_r.at[k * zn + d], z_dev(d))
+            d: rcopy(zsend.at[k, planes.index(d)], zrecv.at[k, d], zr_s.at[k * zn + d], zr_r.at[k * zn + d], z_dev(d))
             for d in ring
         }
 
@@ -309,19 +308,21 @@
         for copy in z_copies(k).values():
             copy.start()
 
-    mine = iota((kr, LANES), 1) == iota((kr, LANES), 0) + z * kr
-
     def settle(k, copies):
         received(copies)
-        parts = [zsend[k, z]] + [zrecv[k, d] for d in range(1, zn)]
-        stats = [stat_row(part[kr : 2 * kr, :]) for part in parts]
-        top = functools.reduce(jnp.maximum, stats)
-        weights = [jnp.exp2(st - top) for st in stats]
+        parts = [zsend[k, 0]] + [zrecv[k, d] for d in range(1, zn)]
+        columns = []
+        for d in range(zn):
+            mine = iota((kr, LANES), 1) == iota((kr, LANES), 0) + planes.index(d) * kr
+            columns.append(
+                jnp.sum(jnp.where(mine, stat_row(parts[d][kr : 2 * kr, :]), 0.0), axis=1, keepdims=True)
+            )
+        top = functools.reduce(jnp.maximum, columns)
+        weights = [jnp.exp2(column - top) for column in columns]
         inverse = 1.0 / functools.reduce(jnp.add, weights)
         acc = jnp.zeros((kr, HD), F32)
         for d in range(zn):
-            column = jnp.sum(jnp.where(mine, weights[d] * inverse, 0.0), axis=1, keepdims=True)
-            acc = acc + column * parts[d][0:kr, :].astype(F32)
+            acc = acc + (weights[d] * inverse) * parts[d][0:kr, :].astype(F32)
         hz[k, pl.ds(z, 1)] = acc.astype(BF16)[None]
         return z_group(
             lambda d: rcopy(hz.at[k, z], hz.at[k, z], hz_s.at[k * zn + d], hz_r.at[k * zn + d], z_dev(d))
@@ -334,7 +335,7 @@
             hall[k, pl.ds(b, 1), :, h * HD : (h + 1) * HD] = pieces[h * tb : (h + 1) * tb, :][None]
         copies = {
             i: rcopy(hall.at[k, b], hall.at[k, b], h2_s.at[k * nb + i], h2_r.at[k * nb + i], plus_dev(i))
-            for i in range(1, nb)
+            for i in far_first
         }
         for copy in copies.values():
             copy.start()
@@ -367,13 +368,12 @@
                     adp[first : first + LANES, h * HD : (h + 1) * HD].astype(F32).T.astype(BF16)
                 )
 
-    score(0, 0, 1, sbuf[0])
-    score(1, 0, 1, sbuf[1])
-    weigh(0, 0, 1, sbuf[0])
-    queries_here(0, *units[0])
-    score(0, *units[0], sbuf[0])
-    weigh(1, 0, 1, sbuf[1])
-    lax.fori_loop(0, kvl, attend, 0)
+    attend([(0, k, 0, 1) for k in range(kvl)])
+    pass_on(1)
+    pairs = [(1, 1)] + [(i, 2) for i in range(2, nb, 2)]
+    attend([(0, k, i, count) for k in range(kvl) for i, count in pairs])
+    quads = [(nb // 2, nb // 2), (0, nb // 2)]
+    attend([(1, k, i, count) for k in range(kvl) for i, count in quads], 2 * kvl - 1)
 
     regroup_h[...] = regroup(GROUP, zn)
     received(zc)
@@ -417,7 +417,8 @@
     sent(za, z_copies(0), z_copies(1), c2)
     for j in range(kvl * nb):
         if j % nb:
-            q_copy(j, j % nb).wait_send()
+            q_copy(0, j, j % nb).wait_send()
+            q_copy(1, j, j % nb).wait_send()
             o_copy(j, j % nb).wait_send()
     g1 = spread(1, h1)
     project(0, g0)
@@ -454,7 +455,7 @@
         for d in range(nb):
             st1s[d, 0:2, j * LANES : (j + 1) * LANES] = out[2 * d : 2 * d + 2, :]
     s1 = {}
-    for i in range(1, nb):
+    for i in far_first:
         py, px = plus(i)
         s1[i] = rcopy(st1s.at[py * xn + px], st1r.at[b], s1_s.at[i], s1_r.at[i], at(py, z, px))
         s1[i].start()
@@ -489,6 +490,8 @@
     cpd = adapter.shape[0]
     aw = zn * xn * cpd
     groups = cotangent.shape[1] // LANES
+    near = 1 + 2 * (zn // 4)
+    buf_rows = kr * max(2 * near, nb // 2 * (zn - near))
     vm = pltpu.VMEM
     dma = pltpu.SemaphoreType.DMA
     scratch = [
@@ -510,8 +513,9 @@
         vm((rows, aw), F32),
         vm((rows, HD), F32),
         vm((heads, cpd + 8 + 2 * nb * (aw // LANES), max(rows, LANES)), F32),
-        vm((2 * zn * kr, positions), F32),
-        vm((2 * zn * kr, positions), F32),
+        vm((buf_rows, positions), F32),
+        vm((buf_rows, positions), F32),
+        vm((kvl * nb, LANES), F32),
         vm((zn * kr, zn * kr), BF16),
         vm((zn, groups * 2, LANES), BF16),
         vm((groups, tb, LANES), BF16),
@@ -523,7 +527,7 @@
         vm((aw, nf), BF16),
         vm((nf, aw), BF16),
         dma((6 + kvl,)),
-        dma((kvl * zn,)), dma((kvl * zn,)), dma((kvl * nb,)), dma((kvl * nb,)),
+        dma((kvl * zn,)), dma((kvl * zn,)), dma((2 * kvl * nb,)), dma((2 * kvl * nb,)),
         dma((zn,)), dma((zn,)), dma((nb,)), dma((nb,)),
         dma((kvl * nb,)), dma((kvl * nb,)),
         dma((kvl * zn,)), dma((kvl * zn,)), dma((kvl * zn,)), dma((kvl * zn,)),

time: 59.2 us -> 62.7 us (1.059)
  Pallas kernels: 57.1 us -> 60.7 us
    pallas_call x1, Pallas kernels: 57.1 us -> 60.7 us  [local(): pl.pallas_call(functools.partial(kernel, sizes, heads, float(heads * nf))...]
where the time goes in v6:
time: 62.7 us; the launch traced here: 62.6 us
  Pallas kernels  60.7 us (97%)
  local copies, waits for them, and re-layouts  1.26 us (2%)
  between operations  0.64 us (1%)
    pallas_call x1, Pallas kernels, local(): pl.pallas_call(functools.partial(kernel, sizes, heads, float(heads * nf))...  60.7 us
    unnamed x2, local copies, waits for them, and re-layouts  1.26 us

profile of v6, /device:TPU:1, one launch (start us, length us, event | category | flops | bytes accessed | tf_op | source)
XLA Modules:
  0.0 62.6 jit_solution(9777760722278945461)
XLA Ops:
  0.6 60.7 %distill.1 = (f32[2,1024]{1,0:T(2,128)S(1)}, f32[16,2048]{1,0:T(8,128)S(1)}) custom-call(bf16[2,2048]{1,0:T(2,128)(2,1)} %q_hbm.1, bf16[2048,256]{1,0:T(8,128)(2,1)} %k_hbm.1, bf16[2048,256]{1,0:T(8,128)(2,1)} %v_hbm.1, bf16[16,128]{1,0:T(8,128)(2,1)} %bitcast.2, bf16[16,2048]{1,0:T(8,128)(2,1)} %ad_hbm.1, s32[1,128]{1,0:T(1,128)} %bitcast.3, ...), custom_call_target="tpu_custom_call" | custom-call | flops 2147483648 | bytes 2097152 | tf_op jit(solution)/shard_map/distill/pallas_call | solution.py:541
  61.3 0.6 copy.11
  61.9 0.7 %copy.12 = f32[16,2048]{1,0:T(8,128)} copy(f32[16,2048]{1,0:T(8,128)S(1)} %get-tuple-element.3) | data formatting | bytes 262144

commit v7 on v5

--- a/solution.py
+++ b/solution.py
@@ -94,24 +94,15 @@
     def z_dev(d):
         return at(y, z_plus(d), x)
 
-    def steps(i):
-        far, turn = div(i, yn), mod(i, yn)
-        if isinstance(i, int):
-            near = (0, 1, 3, 2)[turn] if yn == 4 else turn
-            return (near if far == 0 else (2, 1, 3, 0)[turn] if yn == 4 else yn - 1 - turn), far
-        if yn == 4:
-            first = jnp.where(turn == 2, 3, jnp.where(turn == 3, 2, turn))
-            second = jnp.where(turn == 0, 2, jnp.where(turn == 1, 1, jnp.where(turn == 2, 3, 0)))
-        else:
-            first, second = turn, yn - 1 - turn
-        return jnp.where(far == 0, first, second), far
+    others = [(dy, dx) for dy in range(yn) for dx in range(xn) if dy or dx]
+    steps = [(0, 0)] + sorted(others, key=lambda st: (-min(st[0], yn - st[0]) - st[1], -st[1], st[0]))
 
     def plus(i):
-        dy, dx = steps(i)
+        dy, dx = steps[i]
         return mod(y + dy, yn), mod(x + dx, xn)
 
     def minus(i):
-        dy, dx = steps(i)
+        dy, dx = steps[i]
         return mod(y + yn - dy, yn), mod(x + xn - dx, xn)
 
     def plus_dev(i):
@@ -254,7 +245,7 @@
     def o_copy(j, i):
         return rcopy(osend.at[j], orecv.at[j], o_s.at[j], o_r.at[j], minus_dev(i))
 
-    units = [(1, 1)] + [(i, 2) for i in range(2, nb, 2)]
+    units = [(1, nb // 2 - 1), (nb // 2, nb // 2)]
 
     def queries_here(k, i, count):
         for c in range(count):
@@ -268,10 +259,6 @@
                 score(k, *units[n + 1], there)
                 weigh(k, i, count, here)
             else:
-
-                @pl.when(k == 1)
-                def _():
-                    combine(0)
 
                 later = jnp.minimum(k + 1, kvl - 1)
 
@@ -342,7 +329,7 @@
 
     def project(k, copies):
         gain = gain_ref[...].astype(F32)
-        for i in range(nb):
+        for i in (0, *range(nb - 1, 0, -1)):
             if i > 0:
                 copies[i].wait_recv()
             my, mx = minus(i)
@@ -388,6 +375,7 @@
         c2[i].start()
     call[pl.ds(b, 1)] = cg[pl.ds(my_group, 1)]
 
+    combine(0)
     combine(1)
     sent(*zq, zc)
     h0 = settle(0, z_copies(0))
@@ -510,8 +498,8 @@
         vm((rows, aw), F32),
         vm((rows, HD), F32),
         vm((heads, cpd + 8 + 2 * nb * (aw // LANES), max(rows, LANES)), F32),
-        vm((2 * zn * kr, positions), F32),
-        vm((2 * zn * kr, positions), F32),
+        vm((nb // 2 * zn * kr, positions), F32),
+        vm((nb // 2 * zn * kr, positions), F32),
         vm((zn * kr, zn * kr), BF16),
         vm((zn, groups * 2, LANES), BF16),
         vm((groups, tb, LANES), BF16),

time: 59.2 us -> 56.7 us (0.958)
  Pallas kernels: 57.1 us -> 54.7 us
    pallas_call x1, Pallas kernels: 57.1 us -> 54.7 us  [local(): pl.pallas_call(functools.partial(kernel, sizes, heads, float(heads * nf))...]
where the time goes in v7:
time: 56.7 us; the launch traced here: 56.6 us
  Pallas kernels  54.7 us (96%)
  local copies, waits for them, and re-layouts  1.26 us (2%)
  between operations  0.64 us (1%)
    pallas_call x1, Pallas kernels, local(): pl.pallas_call(functools.partial(kernel, sizes, heads, float(heads * nf))...  54.7 us
    unnamed x2, local copies, waits for them, and re-layouts  1.26 us

profile of v7, /device:TPU:1, one launch (start us, length us, event | category | flops | bytes accessed | tf_op | source)
XLA Modules:
  0.0 56.6 jit_solution(5353486302810322444)
XLA Ops:
  0.6 54.7 %distill.1 = (f32[2,1024]{1,0:T(2,128)S(1)}, f32[16,2048]{1,0:T(8,128)S(1)}) custom-call(bf16[2,2048]{1,0:T(2,128)(2,1)} %q_hbm.1, bf16[2048,256]{1,0:T(8,128)(2,1)} %k_hbm.1, bf16[2048,256]{1,0:T(8,128)(2,1)} %v_hbm.1, bf16[16,128]{1,0:T(8,128)(2,1)} %bitcast.2, bf16[16,2048]{1,0:T(8,128)(2,1)} %ad_hbm.1, s32[1,128]{1,0:T(1,128)} %bitcast.3, ...), custom_call_target="tpu_custom_call" | custom-call | flops 2147483648 | bytes 2097152 | tf_op jit(solution)/shard_map/distill/pallas_call | solution.py:525
  55.4 0.6 %copy.11 = f32[2,1024]{1,0:T(2,128)} copy(f32[2,1024]{1,0:T(2,128)S(1)} %get-tuple-element.2) | data formatting | bytes 16384
  56.0 0.7 %copy.12 = f32[16,2048]{1,0:T(8,128)} copy(f32[16,2048]{1,0:T(8,128)S(1)} %get-tuple-element.3) | data formatting | bytes 262144

commit v8 on v7

--- a/solution.py
+++ b/solution.py
@@ -149,7 +149,7 @@
     q_load.wait()
     qf = q_ref[...].astype(F32)
     for k in range(kvl):
-        qall[k * nb, pl.ds(z, 1)] = jnp.concatenate(
+        qall[k, 0, pl.ds(z, 1)] = jnp.concatenate(
             [qf[:, (k * GROUP + h) * HD : (k * GROUP + h + 1) * HD] for h in range(GROUP)], axis=0
         ).astype(BF16)[None]
     cot_load.wait()
@@ -174,14 +174,7 @@
             for copy in copies.values():
                 copy.wait_send()
 
-    zq = [
-        z_group(
-            lambda d, k=k: rcopy(
-                qall.at[k * nb, z], qall.at[k * nb, z], zq_s.at[k * zn + d], zq_r.at[k * zn + d], z_dev(d)
-            )
-        )
-        for k in range(kvl)
-    ]
+    zq = z_group(lambda d: rcopy(qall.at[:, 0, z], qall.at[:, 0, z], zq_s.at[d], zq_r.at[d], z_dev(d)))
     zc = z_group(lambda d: rcopy(cz.at[z], cz.at[z], zc_s.at[d], zc_r.at[d], z_dev(d)))
 
     k_load.wait()
@@ -190,13 +183,13 @@
     for k in range(kvl):
         vaug[k, :, HD : 2 * HD] = jnp.ones((vaug.shape[1], HD), BF16)
 
-    def q_copy(j, i):
-        return rcopy(qall.at[j - i], qall.at[j], q2_s.at[j], q2_r.at[j], plus_dev(i))
-
+    def q_copy(k, i):
+        return rcopy(qall.at[k, 0], qall.at[k, i], q2_s.at[k * nb + i], q2_r.at[k * nb + i], plus_dev(i))
+
+    received(zq)
     for k in range(kvl):
-        received(zq[k])
         for i in range(1, nb):
-            q_copy(k * nb + i, i).start()
+            q_copy(k, i).start()
 
     for d in range(zn):
         for e in range(1, xn):
@@ -223,7 +216,7 @@
         return wide[0:1, :] + wide[1:2, :] + wide[2:3, :]
 
     def score(k, i, count, buf):
-        q = qall[pl.ds(k * nb + i, count)].reshape(count * qrows, HD)
+        q = qall[k, i : i + count].reshape(count * qrows, HD)
         buf[0 : count * qrows, :] = nn(q, k_t[k])
 
     def weigh(k, i, count, buf):
@@ -249,7 +242,7 @@
 
     def queries_here(k, i, count):
         for c in range(count):
-            q_copy(k * nb + i + c, i + c).wait_recv()
+            q_copy(k, i + c).wait_recv()
 
     def attend(k, carry):
         for n, (i, count) in enumerate(units):
@@ -357,9 +350,9 @@
     score(0, 0, 1, sbuf[0])
     score(1, 0, 1, sbuf[1])
     weigh(0, 0, 1, sbuf[0])
+    weigh(1, 0, 1, sbuf[1])
     queries_here(0, *units[0])
     score(0, *units[0], sbuf[0])
-    weigh(1, 0, 1, sbuf[1])
     lax.fori_loop(0, kvl, attend, 0)
 
     regroup_h[...] = regroup(GROUP, zn)
@@ -377,7 +370,7 @@
 
     combine(0)
     combine(1)
-    sent(*zq, zc)
+    sent(zq, zc)
     h0 = settle(0, z_copies(0))
     received(za)
     turn_adapter(0)
@@ -405,7 +398,7 @@
     sent(za, z_copies(0), z_copies(1), c2)
     for j in range(kvl * nb):
         if j % nb:
-            q_copy(j, j % nb).wait_send()
+            q_copy(j // nb, j % nb).wait_send()
             o_copy(j, j % nb).wait_send()
     g1 = spread(1, h1)
     project(0, g0)
@@ -487,7 +480,7 @@
         vm((positions, kvw), BF16),
         vm((kvl, HD, positions), BF16),
         vm((kvl, positions, 2 * HD), BF16),
-        vm((kvl * nb, zn, kr, HD), BF16),
+        vm((kvl, nb, zn, kr, HD), BF16),
         vm((kvl * nb, zn + 1, kr, HD), BF16),
         vm((kvl * nb, zn + 1, kr, HD), BF16),
         vm((kvl, zn, 2 * kr, HD), BF16),
@@ -511,7 +504,7 @@
         vm((aw, nf), BF16),
         vm((nf, aw), BF16),
         dma((6 + kvl,)),
-        dma((kvl * zn,)), dma((kvl * zn,)), dma((kvl * nb,)), dma((kvl * nb,)),
+        dma((zn,)), dma((zn,)), dma((kvl * nb,)), dma((kvl * nb,)),
         dma((zn,)), dma((zn,)), dma((nb,)), dma((nb,)),
         dma((kvl * nb,)), dma((kvl * nb,)),
         dma((kvl * zn,)), dma((kvl * zn,)), dma((kvl * zn,)), dma((kvl * zn,)),

time: 56.7 us -> 56.9 us (level)
  no operation moved by 1% of the time
where the time goes in v8:
time: 56.9 us; the launch traced here: 56.7 us
  Pallas kernels  54.8 us (96%)
  local copies, waits for them, and re-layouts  1.26 us (2%)
  between operations  0.64 us (1%)
    pallas_call x1, Pallas kernels, local(): pl.pallas_call(functools.partial(kernel, sizes, heads, float(heads * nf))...  54.8 us
    unnamed x2, local copies, waits for them, and re-layouts  1.26 us

profile of v8, /device:TPU:1, one launch (start us, length us, event | category | flops | bytes accessed | tf_op | source)
XLA Modules:
  0.0 56.7 jit_solution(15004055502501981390)
XLA Ops:
  0.6 54.8 %distill.1 = (f32[2,1024]{1,0:T(2,128)S(1)}, f32[16,2048]{1,0:T(8,128)S(1)}) custom-call(bf16[2,2048]{1,0:T(2,128)(2,1)} %q_hbm.1, bf16[2048,256]{1,0:T(8,128)(2,1)} %k_hbm.1, bf16[2048,256]{1,0:T(8,128)(2,1)} %v_hbm.1, bf16[16,128]{1,0:T(8,128)(2,1)} %bitcast.2, bf16[16,2048]{1,0:T(8,128)(2,1)} %ad_hbm.1, s32[1,128]{1,0:T(1,128)} %bitcast.3, ...), custom_call_target="tpu_custom_call" | custom-call | flops 2147483648 | bytes 2097152 | tf_op jit(solution)/shard_map/distill/pallas_call | solution.py:518
  55.5 0.6 %copy.11 = f32[2,1024]{1,0:T(2,128)} copy(f32[2,1024]{1,0:T(2,128)S(1)} %get-tuple-element.2) | data formatting | bytes 16384
  56.1 0.7 %copy.12 = f32[16,2048]{1,0:T(8,128)} copy(f32[16,2048]{1,0:T(8,128)S(1)} %get-tuple-element.3) | data formatting | bytes 262144

commit v9 on v8

--- a/solution.py
+++ b/solution.py
@@ -238,30 +238,14 @@
     def o_copy(j, i):
         return rcopy(osend.at[j], orecv.at[j], o_s.at[j], o_r.at[j], minus_dev(i))
 
-    units = [(1, nb // 2 - 1), (nb // 2, nb // 2)]
-
-    def queries_here(k, i, count):
+    half = nb // 2
+    units = [(0, 1, half - 1), (0, half, half), (1, 1, half), (1, half + 1, half - 1)]
+
+    def begin(n):
+        k, i, count = units[n]
         for c in range(count):
             q_copy(k, i + c).wait_recv()
-
-    def attend(k, carry):
-        for n, (i, count) in enumerate(units):
-            here, there = sbuf[n % 2], sbuf[(n + 1) % 2]
-            if n + 1 < len(units):
-                queries_here(k, *units[n + 1])
-                score(k, *units[n + 1], there)
-                weigh(k, i, count, here)
-            else:
-
-                later = jnp.minimum(k + 1, kvl - 1)
-
-                @pl.when(k + 1 < kvl)
-                def _():
-                    queries_here(later, *units[0])
-
-                score(later, *units[0], there)
-                weigh(k, i, count, here)
-        return carry
+        score(*units[n], sbuf[n % 2])
 
     def z_copies(k):
         return {
@@ -351,9 +335,11 @@
     score(1, 0, 1, sbuf[1])
     weigh(0, 0, 1, sbuf[0])
     weigh(1, 0, 1, sbuf[1])
-    queries_here(0, *units[0])
-    score(0, *units[0], sbuf[0])
-    lax.fori_loop(0, kvl, attend, 0)
+    begin(0)
+    for n, unit in enumerate(units):
+        if n + 1 < len(units):
+            begin(n + 1)
+        weigh(*unit, sbuf[n % 2])
 
     regroup_h[...] = regroup(GROUP, zn)
     received(zc)

time: 56.9 us -> 57.5 us (1.011)
  Pallas kernels: 54.8 us -> 55.5 us
    pallas_call x1, Pallas kernels: 54.8 us -> 55.5 us  [local(): pl.pallas_call(functools.partial(kernel, sizes, heads, float(heads * nf))...]
where the time goes in v9:
time: 57.5 us; the launch traced here: 57.4 us
  Pallas kernels  55.5 us (97%)
  local copies, waits for them, and re-layouts  1.26 us (2%)
  between operations  0.64 us (1%)
    pallas_call x1, Pallas kernels, local(): pl.pallas_call(functools.partial(kernel, sizes, heads, float(heads * nf))...  55.5 us
    unnamed x2, local copies, waits for them, and re-layouts  1.26 us

profile of v9, /device:TPU:1, one launch (start us, length us, event | category | flops | bytes accessed | tf_op | source)
XLA Modules:
  0.0 57.4 jit_solution(12867111525391587510)
XLA Ops:
  0.6 55.5 %distill.1 = (f32[2,1024]{1,0:T(2,128)S(1)}, f32[16,2048]{1,0:T(8,128)S(1)}) custom-call(bf16[2,2048]{1,0:T(2,128)(2,1)} %q_hbm.1, bf16[2048,256]{1,0:T(8,128)(2,1)} %k_hbm.1, bf16[2048,256]{1,0:T(8,128)(2,1)} %v_hbm.1, bf16[16,128]{1,0:T(8,128)(2,1)} %bitcast.2, bf16[16,2048]{1,0:T(8,128)(2,1)} %ad_hbm.1, s32[1,128]{1,0:T(1,128)} %bitcast.3, ...), custom_call_target="tpu_custom_call" | custom-call | flops 2147483648 | bytes 2097152 | tf_op jit(solution)/shard_map/distill/pallas_call | solution.py:504
  56.1 0.6 %copy.11 = f32[2,1024]{1,0:T(2,128)} copy(f32[2,1024]{1,0:T(2,128)S(1)} %get-tuple-element.2) | data formatting | bytes 16384
  56.7 0.7 %copy.12 = f32[16,2048]{1,0:T(8,128)} copy(f32[16,2048]{1,0:T(8,128)S(1)} %get-tuple-element.3) | data formatting | bytes 262144

commit v10 on v8

--- a/solution.py
+++ b/solution.py
@@ -58,7 +58,7 @@
 
 def kernel(sizes, heads, eps_div, q_hbm, k_hbm, v_hbm, gain_hbm, ad_hbm, src_hbm, cot_hbm,
            stu_ref, grad_ref,
-           q_ref, gain_ref, src_ref, cot_ref, kbuf, k_t, vaug, qall, osend, orecv, zsend, zrecv,
+           q_ref, gain_ref, src_ref, cot_ref, kbuf, k_t, v_own, qall, osend, orecv, zsend, zrecv,
            hz, hall, gall, mpre, squares, hx, s_even, s_odd, regroup_h, cz, cg, call, cot_t, mpre_t, st1s, st1r,
            adp, ad_t,
            loc_sem, zq_s, zq_r, q2_s, q2_r, zc_s, zc_r, c2_s, c2_r, o_s, o_r,
@@ -140,7 +140,7 @@
     for k in range(kvl):
         late_loads.append(
             pltpu.make_async_copy(
-                v_hbm.at[:, k * HD : (k + 1) * HD], vaug.at[k, :, 0:HD], loc_sem.at[6 + k]
+                v_hbm.at[:, k * HD : (k + 1) * HD], v_own.at[k], loc_sem.at[6 + k]
             )
         )
     for load in [cot_load, k_load, ad_load] + late_loads:
@@ -180,8 +180,6 @@
     k_load.wait()
     for k in range(kvl):
         k_t[k] = kbuf[:, k * HD : (k + 1) * HD].astype(F32).T.astype(BF16)
-    for k in range(kvl):
-        vaug[k, :, HD : 2 * HD] = jnp.ones((vaug.shape[1], HD), BF16)
 
     def q_copy(k, i):
         return rcopy(qall.at[k, 0], qall.at[k, i], q2_s.at[k * nb + i], q2_r.at[k * nb + i], plus_dev(i))
@@ -222,10 +220,9 @@
     def weigh(k, i, count, buf):
         s = buf[0 : count * qrows, :]
         m = jnp.max(s, axis=1, keepdims=True)
-        p = jnp.exp2((buf[0 : count * qrows, :] - m) * factor).astype(BF16)
-        oa = nn(p, vaug[k])
-        total = oa[:, HD : 2 * HD]
-        o = (oa[:, 0:HD] / total).astype(BF16)
+        p = jnp.exp2((buf[0 : count * qrows, :] - m) * factor)
+        total = jnp.sum(p, axis=1, keepdims=True)
+        o = (nn(p.astype(BF16), v_own[k]) * (1.0 / total)).astype(BF16)
         lse = m * factor + jnp.log2(total)
         for c in range(count):
             part = slice(c * qrows, (c + 1) * qrows)
@@ -347,10 +344,12 @@
                     adp[first : first + LANES, h * HD : (h + 1) * HD].astype(F32).T.astype(BF16)
                 )
 
-    score(0, 0, 1, sbuf[0])
-    score(1, 0, 1, sbuf[1])
-    weigh(0, 0, 1, sbuf[0])
-    weigh(1, 0, 1, sbuf[1])
+    def attend_own(k, carry):
+        score(k, 0, 1, sbuf[0])
+        weigh(k, 0, 1, sbuf[0])
+        return carry
+
+    lax.fori_loop(0, kvl, attend_own, 0)
     queries_here(0, *units[0])
     score(0, *units[0], sbuf[0])
     lax.fori_loop(0, kvl, attend, 0)
@@ -479,7 +478,7 @@
         vm(cotangent.shape, BF16),
         vm((positions, kvw), BF16),
         vm((kvl, HD, positions), BF16),
-        vm((kvl, positions, 2 * HD), BF16),
+        vm((kvl, positions, HD), BF16),
         vm((kvl, nb, zn, kr, HD), BF16),
         vm((kvl * nb, zn + 1, kr, HD), BF16),
         vm((kvl * nb, zn + 1, kr, HD), BF16),

time: 56.9 us -> 57.9 us (1.018)
  Pallas kernels: 54.8 us -> 55.9 us
    pallas_call x1, Pallas kernels: 54.8 us -> 55.9 us  [local(): pl.pallas_call(functools.partial(kernel, sizes, heads, float(heads * nf))...]
where the time goes in v10:
time: 57.9 us; the launch traced here: 57.8 us
  Pallas kernels  55.9 us (97%)
  local copies, waits for them, and re-layouts  1.26 us (2%)
  between operations  0.64 us (1%)
    pallas_call x1, Pallas kernels, local(): pl.pallas_call(functools.partial(kernel, sizes, heads, float(heads * nf))...  55.9 us
    unnamed x2, local copies, waits for them, and re-layouts  1.26 us

profile of v10, /device:TPU:1, one launch (start us, length us, event | category | flops | bytes accessed | tf_op | source)
XLA Modules:
  0.0 57.8 jit_solution(4485509232968425654)
XLA Ops:
  0.6 55.9 %distill.1 = (f32[2,1024]{1,0:T(2,128)S(1)}, f32[16,2048]{1,0:T(8,128)S(1)}) custom-call(bf16[2,2048]{1,0:T(2,128)(2,1)} %q_hbm.1, bf16[2048,256]{1,0:T(8,128)(2,1)} %k_hbm.1, bf16[2048,256]{1,0:T(8,128)(2,1)} %v_hbm.1, bf16[16,128]{1,0:T(8,128)(2,1)} %bitcast.2, bf16[16,2048]{1,0:T(8,128)(2,1)} %ad_hbm.1, s32[1,128]{1,0:T(1,128)} %bitcast.3, ...), custom_call_target="tpu_custom_call" | custom-call | flops 2147483648 | bytes 2097152 | tf_op jit(solution)/shard_map/distill/pallas_call | solution.py:517
  56.5 0.6 %copy.11 = f32[2,1024]{1,0:T(2,128)} copy(f32[2,1024]{1,0:T(2,128)S(1)} %get-tuple-element.2) | data formatting | bytes 16384
  57.1 0.7 %copy.12 = f32[16,2048]{1,0:T(8,128)} copy(f32[16,2048]{1,0:T(8,128)S(1)} %get-tuple-element.3) | data formatting | bytes 262144

commit v11 on v8

--- a/solution.py
+++ b/solution.py
@@ -205,15 +205,16 @@
     qrows = zn * kr
     eye = iota((qrows, LANES), 0) == iota((qrows, LANES), 1)
 
-    def stat_tile(row):
-        high, middle, low = split3(row)
-        line = iota((kr, LANES), 0)
-        tile = jnp.where(line == 0, high.astype(F32), jnp.where(line == 1, middle.astype(F32), low.astype(F32)))
-        return jnp.where(line < 3, tile, 0.0).astype(BF16)
-
-    def stat_row(tile):
+    def stat_tile(*lines):
+        at_line = iota((kr, LANES), 0)
+        tile = jnp.zeros((kr, LANES), F32)
+        for n, term in enumerate(term for line in lines for term in split3(line)):
+            tile = jnp.where(at_line == n, term.astype(F32), tile)
+        return tile.astype(BF16)
+
+    def stat_row(tile, n=0):
         wide = tile.astype(F32)
-        return wide[0:1, :] + wide[1:2, :] + wide[2:3, :]
+        return wide[3 * n : 3 * n + 1, :] + wide[3 * n + 1 : 3 * n + 2, :] + wide[3 * n + 2 : 3 * n + 3, :]
 
     def score(k, i, count, buf):
         q = qall[k, i : i + count].reshape(count * qrows, HD)
@@ -225,13 +226,14 @@
         p = jnp.exp2((buf[0 : count * qrows, :] - m) * factor).astype(BF16)
         oa = nn(p, vaug[k])
         total = oa[:, HD : 2 * HD]
-        o = (oa[:, 0:HD] / total).astype(BF16)
-        lse = m * factor + jnp.log2(total)
+        o = oa[:, 0:HD].astype(BF16)
         for c in range(count):
             part = slice(c * qrows, (c + 1) * qrows)
             osend[k * nb + i + c, 0:zn] = o[part].reshape(zn, kr, HD)
-            row = jnp.sum(jnp.where(eye, lse[part], 0.0), axis=0, keepdims=True)
-            osend[k * nb + i + c, zn] = stat_tile(row)
+            top, weight = (
+                jnp.sum(jnp.where(eye, column[part], 0.0), axis=0, keepdims=True) for column in (m, total)
+            )
+            osend[k * nb + i + c, zn] = stat_tile(top * factor, weight)
             if i + c > 0:
                 o_copy(k * nb + i + c, i + c).start()
 
@@ -276,7 +278,9 @@
         stats = [stat_row(part[zn]) for part in parts]
         top = functools.reduce(jnp.maximum, stats)
         weights = [jnp.exp2(st - top) for st in stats]
-        weight_sum = functools.reduce(jnp.add, weights)
+        weight_sum = functools.reduce(
+            jnp.add, [weight * stat_row(part[zn], 1) for weight, part in zip(weights, parts)]
+        )
         inverse = 1.0 / weight_sum
         acc = jnp.zeros((qrows, HD), F32)
         for i in range(nb):

time: 56.9 us -> 57 us (level)
  no operation moved by 1% of the time
where the time goes in v11:
time: 57 us; the launch traced here: 56.8 us
  Pallas kernels  54.9 us (96%)
  local copies, waits for them, and re-layouts  1.26 us (2%)
  between operations  0.64 us (1%)
    pallas_call x1, Pallas kernels, local(): pl.pallas_call(functools.partial(kernel, sizes, heads, float(heads * nf))...  54.9 us
    unnamed x2, local copies, waits for them, and re-layouts  1.26 us

profile of v11, /device:TPU:1, one launch (start us, length us, event | category | flops | bytes accessed | tf_op | source)
XLA Modules:
  0.0 56.8 jit_solution(876864147711570582)
XLA Ops:
  0.6 54.9 %distill.1 = (f32[2,1024]{1,0:T(2,128)S(1)}, f32[16,2048]{1,0:T(8,128)S(1)}) custom-call(bf16[2,2048]{1,0:T(2,128)(2,1)} %q_hbm.1, bf16[2048,256]{1,0:T(8,128)(2,1)} %k_hbm.1, bf16[2048,256]{1,0:T(8,128)(2,1)} %v_hbm.1, bf16[16,128]{1,0:T(8,128)(2,1)} %bitcast.2, bf16[16,2048]{1,0:T(8,128)(2,1)} %ad_hbm.1, s32[1,128]{1,0:T(1,128)} %bitcast.3, ...), custom_call_target="tpu_custom_call" | custom-call | flops 2147483648 | bytes 2097152 | tf_op jit(solution)/shard_map/distill/pallas_call | solution.py:522
  55.6 0.6 %copy.11 = f32[2,1024]{1,0:T(2,128)} copy(f32[2,1024]{1,0:T(2,128)S(1)} %get-tuple-element.2) | data formatting | bytes 16384
  56.2 0.7 %copy.12 = f32[16,2048]{1,0:T(8,128)} copy(f32[16,2048]{1,0:T(8,128)S(1)} %get-tuple-element.3) | data formatting | bytes 262144

commit v12 on v8

--- a/solution.py
+++ b/solution.py
@@ -118,6 +118,13 @@
             src_ref=src, dst_ref=dst, send_sem=ssem, recv_sem=rsem, device_id=dev, device_id_type=MESH
         )
 
+    def loop(first, last, body):
+        def step(n, carry):
+            body(n)
+            return carry
+
+        lax.fori_loop(first, last, step, 0)
+
     q_load = pltpu.make_async_copy(q_hbm, q_ref, loc_sem.at[0])
     q_load.start()
     barrier = pltpu.get_barrier_semaphore()
@@ -178,8 +185,13 @@
     zc = z_group(lambda d: rcopy(cz.at[z], cz.at[z], zc_s.at[d], zc_r.at[d], z_dev(d)))
 
     k_load.wait()
-    for k in range(kvl):
-        k_t[k] = kbuf[:, k * HD : (k + 1) * HD].astype(F32).T.astype(BF16)
+
+    def turn_keys(c):
+        lines = pl.ds(pl.multiple_of(c * LANES, LANES), LANES)
+        for k in range(kvl):
+            k_t[k, :, lines] = kbuf[lines, k * HD : (k + 1) * HD].astype(F32).T.astype(BF16)
+
+    loop(0, kbuf.shape[0] // LANES, turn_keys)
     for k in range(kvl):
         vaug[k, :, HD : 2 * HD] = jnp.ones((vaug.shape[1], HD), BF16)
 
@@ -341,16 +353,18 @@
         mpre[...] = part if k == 0 else mpre[...] + part
 
     def turn_adapter(k):
-        for h in range(k * GROUP, (k + 1) * GROUP):
+        def turn(h):
+            lanes = pl.ds(pl.multiple_of(h * HD, HD), HD)
             for first in range(0, aw, LANES):
-                ad_t[h * HD : (h + 1) * HD, first : first + LANES] = (
-                    adp[first : first + LANES, h * HD : (h + 1) * HD].astype(F32).T.astype(BF16)
-                )
-
-    score(0, 0, 1, sbuf[0])
-    score(1, 0, 1, sbuf[1])
-    weigh(0, 0, 1, sbuf[0])
-    weigh(1, 0, 1, sbuf[1])
+                ad_t[lanes, first : first + LANES] = adp[first : first + LANES, lanes].astype(F32).T.astype(BF16)
+
+        loop(k * GROUP, (k + 1) * GROUP, turn)
+
+    def attend_own(k):
+        score(k, 0, 1, sbuf[0])
+        weigh(k, 0, 1, sbuf[0])
+
+    loop(0, kvl, attend_own)
     queries_here(0, *units[0])
     score(0, *units[0], sbuf[0])
     lax.fori_loop(0, kvl, attend, 0)

time: 56.9 us -> 56.9 us (level)
  no operation moved by 1% of the time
where the time goes in v12:
time: 56.9 us; the launch traced here: 56.7 us
  Pallas kernels  54.9 us (96%)
  local copies, waits for them, and re-layouts  1.26 us (2%)
  between operations  0.64 us (1%)
    pallas_call x1, Pallas kernels, local(): pl.pallas_call(functools.partial(kernel, sizes, heads, float(heads * nf))...  54.9 us
    unnamed x2, local copies, waits for them, and re-layouts  1.26 us

profile of v12, /device:TPU:1, one launch (start us, length us, event | category | flops | bytes accessed | tf_op | source)
XLA Modules:
  0.0 56.7 jit_solution(689704327817570904)
XLA Ops:
  0.6 54.9 %distill.1 = (f32[2,1024]{1,0:T(2,128)S(1)}, f32[16,2048]{1,0:T(8,128)S(1)}) custom-call(bf16[2,2048]{1,0:T(2,128)(2,1)} %q_hbm.1, bf16[2048,256]{1,0:T(8,128)(2,1)} %k_hbm.1, bf16[2048,256]{1,0:T(8,128)(2,1)} %v_hbm.1, bf16[16,128]{1,0:T(8,128)(2,1)} %bitcast.2, bf16[16,2048]{1,0:T(8,128)(2,1)} %ad_hbm.1, s32[1,128]{1,0:T(1,128)} %bitcast.3, ...), custom_call_target="tpu_custom_call" | custom-call | flops 2147483648 | bytes 2097152 | tf_op jit(solution)/shard_map/distill/pallas_call | solution.py:532
  55.5 0.6 %copy.11 = f32[2,1024]{1,0:T(2,128)} copy(f32[2,1024]{1,0:T(2,128)S(1)} %get-tuple-element.2) | data formatting | bytes 16384
  56.1 0.7 %copy.12 = f32[16,2048]{1,0:T(8,128)} copy(f32[16,2048]{1,0:T(8,128)S(1)} %get-tuple-element.3) | data formatting | bytes 262144
